TPU v7x, 1024 devices: a whole 4x4x32 slice. The times are simulated.
1024 devices in a mesh: lon: 32 (over z_hi, y, core), lat: 32 (over x, z_lo).
Axes of the slice: x: 4, y: 4, z: 32 (z_hi: 4, z_lo: 8; z = z_hi * 8 + z_lo), core: 2. Of those that a mesh axis runs over, the one named last changes fastest.
Arguments:
- bottom_stratum_count: int32 [256, 4096], P('lat', 'lon'), may hold values from 0 to 32, as said below
- free_elevation: float32 [256, 4096], P('lat', 'lon'), may hold values from -4 to 4
- barotropic_velocity_x: float32 [256, 4096], P('lat', 'lon'), may hold values from -4 to 4
- barotropic_velocity_y: float32 [256, 4096], P('lat', 'lon'), may hold values from -4 to 4
- velocity_along_x: float32 [32, 256, 4096], P(None, 'lat', 'lon'), may hold values from -4 to 4
- velocity_along_y: float32 [32, 256, 4096], P(None, 'lat', 'lon'), may hold values from -4 to 4
- thermal_anomaly: float32 [32, 256, 4096], P(None, 'lat', 'lon'), may hold values from -6 to 6
- haline_anomaly: float32 [32, 256, 4096], P(None, 'lat', 'lon'), may hold values from -6 to 6
Outputs:
- surface_out: float32 [256, 4096], P('lat', 'lon')
- east_out: float32 [256, 4096], P('lat', 'lon')
- north_out: float32 [256, 4096], P('lat', 'lon')
- fresh_velocity_along_x: float32 [32, 256, 4096], P(None, 'lat', 'lon')
- fresh_velocity_along_y: float32 [32, 256, 4096], P(None, 'lat', 'lon')
- fresh_thermal_anomaly: float32 [32, 256, 4096], P(None, 'lat', 'lon')
- fresh_haline_anomaly: float32 [32, 256, 4096], P(None, 'lat', 'lon')
Inputs may be any that keep to these rules, and one draw needn't show every extreme that they name: `bottom_stratum_count`: about three in twenty columns are land (0); the others hold 1 to 32 wet levels, independently from column to column.
All inputs are finite; a program needn't handle non-finite values.
Results may differ from a plain program's by a relative error of at most 0.00002.
Values sent between devices are 32-bit elements; how exact they have to be, the bound alone decides.
A program may use at most 32 MiB of HBM per device.

v0:
```python
import jax
import jax.numpy as jnp
from jax import lax
from jax.sharding import PartitionSpec as P

STRATA_COUNT = 32
SUBCYCLES = 8


wave_coef = 0.45
coriolis = 0.12
diapycnal_factor = 0.2
press_coef = 0.1


def extended(cells, sides, width):
    for axis, dim in sides:
        count = lax.axis_size(axis)
        head = lax.slice_in_dim(cells, 0, width, axis=dim)
        tail = lax.slice_in_dim(cells, cells.shape[dim] - width, cells.shape[dim], axis=dim)
        cells = jnp.concatenate(
            [
                lax.ppermute(tail, axis, [(i, (i + 1) % count) for i in range(count)]),
                cells,
                lax.ppermute(head, axis, [((i + 1) % count, i) for i in range(count)]),
            ],
            axis=dim,
        )
    return cells


def level_above(field):
    return jnp.concatenate([jnp.zeros_like(field[:1]), field[:-1]], axis=0)


def level_below(field):
    return jnp.concatenate([field[1:], jnp.zeros_like(field[:1])], axis=0)


def advance(padded, depth, wet):
    stratum_index, volume_flux_x_side, volume_flux_y_side = padded
    flux_x = depth * volume_flux_x_side
    flux_y = depth * volume_flux_y_side
    inner_level = wet[1:-1, 1:-1] * (
        stratum_index[1:-1, 1:-1]
        - wave_coef * (flux_x[1:-1, 2:] - flux_x[1:-1, :-2] + flux_y[2:, 1:-1] - flux_y[:-2, 1:-1])
    )
    depth_in = depth[2:-2, 2:-2]
    wet_in = wet[2:-2, 2:-2]
    old_x = volume_flux_x_side[2:-2, 2:-2]
    old_y = volume_flux_y_side[2:-2, 2:-2]
    new_x = wet_in * (
        old_x
        - wave_coef * depth_in * (inner_level[1:-1, 2:] - inner_level[1:-1, :-2])
        + coriolis * old_y
    )
    new_y = wet_in * (
        old_y
        - wave_coef * depth_in * (inner_level[2:, 1:-1] - inner_level[:-2, 1:-1])
        - coriolis * old_x
    )
    stratum_index = inner_level[1:-1, 1:-1]
    return (stratum_index, new_x, new_y)


def body(
    bottom_stratum_count,
    free_elevation,
    barotropic_velocity_x,
    barotropic_velocity_y,
    velocity_along_x,
    velocity_along_y,
    thermal_anomaly,
    haline_anomaly,
):
    lat_rows, lon_cols = free_elevation.shape
    deepest = 8
    column_pad = extended(bottom_stratum_count, (("lat", 0), ("lon", 1)), deepest)
    global_rows = (
        lax.axis_index("lat") * lat_rows
        - deepest
        + jnp.arange(lat_rows + 2 * deepest, dtype=jnp.int32)
    )
    inside = (global_rows >= 0) & (global_rows < lat_rows * lax.axis_size("lat"))
    column_pad = jnp.where(inside[:, None], column_pad, 0)
    depth_pad = column_pad.astype(jnp.float32) / STRATA_COUNT
    wet_pad = (column_pad > 0).astype(jnp.float32)
    period = 1
    margin_width = 2 * period
    offset = deepest - margin_width
    depth_win = depth_pad[
        offset : offset + lat_rows + 2 * margin_width, offset : offset + lon_cols + 2 * margin_width
    ]
    wet_win = wet_pad[
        offset : offset + lat_rows + 2 * margin_width, offset : offset + lon_cols + 2 * margin_width
    ]
    state = (free_elevation, barotropic_velocity_x, barotropic_velocity_y)
    for rounds in range(SUBCYCLES // period):
        padded = (
            extended(state[0], (("lat", 0), ("lon", 1)), margin_width),
            extended(state[1], (("lat", 0), ("lon", 1)), margin_width),
            extended(state[2], (("lat", 0), ("lon", 1)), margin_width),
        )
        state = advance(padded, depth_win, wet_win)
    stratum_index, volume_flux_x_side, volume_flux_y_side = state
    column_one = column_pad[
        deepest - 1 : deepest + lat_rows + 1, deepest - 1 : deepest + lon_cols + 1
    ]
    levels = jnp.arange(STRATA_COUNT, dtype=jnp.int32)[:, None, None]
    ocean_cell_indicator = (levels < column_one[None]).astype(jnp.float32)
    middle_ocean_indicator = ocean_cell_indicator[:, 1:-1, 1:-1]
    depth_centre = depth_pad[deepest : deepest + lat_rows, deepest : deepest + lon_cols]
    multiplier_factor = 0.08 + 0.12 * depth_centre
    western_velocity_halo, southern_velocity_halo, thermal_halo_array, haline_halo_array = (
        extended(velocity_along_x, (("lat", 1), ("lon", 2)), 1),
        extended(velocity_along_y, (("lat", 1), ("lon", 2)), 1),
        extended(thermal_anomaly, (("lat", 1), ("lon", 2)), 1),
        extended(haline_anomaly, (("lat", 1), ("lon", 2)), 1),
    )

    def horizontal_diffusion(field):
        centre = field[:, 1:-1, 1:-1]
        total = ocean_cell_indicator[:, 1:-1, 2:] * (
            field[:, 1:-1, 2:] - centre
        ) + ocean_cell_indicator[:, 1:-1, :-2] * (field[:, 1:-1, :-2] - centre)
        return (
            total
            + ocean_cell_indicator[:, 2:, 1:-1] * (field[:, 2:, 1:-1] - centre)
            + ocean_cell_indicator[:, :-2, 1:-1] * (field[:, :-2, 1:-1] - centre)
        )

    def diapycnal_diffusion(field):
        return level_above(middle_ocean_indicator) * (level_above(field) - field) + level_below(
            middle_ocean_indicator
        ) * (level_below(field) - field)

    fresh_thermal_anomaly = middle_ocean_indicator * (
        thermal_anomaly
        + multiplier_factor * horizontal_diffusion(thermal_halo_array)
        + diapycnal_factor * diapycnal_diffusion(thermal_anomaly)
    )
    fresh_haline_anomaly = middle_ocean_indicator * (
        haline_anomaly
        + multiplier_factor * horizontal_diffusion(haline_halo_array)
        + diapycnal_factor * diapycnal_diffusion(haline_anomaly)
    )
    hydrostatic_force = jnp.cumsum(
        ocean_cell_indicator * (-0.8 * thermal_halo_array + 0.6 * haline_halo_array), axis=0
    )
    count = jnp.maximum(bottom_stratum_count, 1).astype(jnp.float32)
    mean_x = jnp.sum(middle_ocean_indicator * velocity_along_x, axis=0) / count
    mean_y = jnp.sum(middle_ocean_indicator * velocity_along_y, axis=0) / count
    press_east = hydrostatic_force[:, 1:-1, 2:] - hydrostatic_force[:, 1:-1, :-2]
    press_north = hydrostatic_force[:, 2:, 1:-1] - hydrostatic_force[:, :-2, 1:-1]
    fresh_velocity_along_x = middle_ocean_indicator * (
        velocity_along_x
        - mean_x
        + volume_flux_x_side
        + multiplier_factor * horizontal_diffusion(western_velocity_halo)
        - press_coef * press_east
        + coriolis * velocity_along_y
    )
    fresh_velocity_along_y = middle_ocean_indicator * (
        velocity_along_y
        - mean_y
        + volume_flux_y_side
        + multiplier_factor * horizontal_diffusion(southern_velocity_halo)
        - press_coef * press_north
        - coriolis * velocity_along_x
    )
    return (
        stratum_index,
        volume_flux_x_side,
        volume_flux_y_side,
        fresh_velocity_along_x,
        fresh_velocity_along_y,
        fresh_thermal_anomaly,
        fresh_haline_anomaly,
    )


def solution(mesh):
    in_specs = (
        P("lat", "lon"),
        P("lat", "lon"),
        P("lat", "lon"),
        P("lat", "lon"),
        P(None, "lat", "lon"),
        P(None, "lat", "lon"),
        P(None, "lat", "lon"),
        P(None, "lat", "lon"),
    )
    out_specs = (
        P("lat", "lon"),
        P("lat", "lon"),
        P("lat", "lon"),
        P(None, "lat", "lon"),
        P(None, "lat", "lon"),
        P(None, "lat", "lon"),
        P(None, "lat", "lon"),
    )
    return jax.shard_map(body, mesh=mesh, in_specs=in_specs, out_specs=out_specs, check_vma=False)
```

profile of v0, /device:TPU:25, one launch (start us, length us, event | category | flops | bytes accessed | tf_op | source)
XLA Modules:
  0.0 945.8 jit_solution(14647198592926054924)
XLA Ops:
  4.2 13.4 %collective-permute-start.1 = (s32[8,128]{1,0:T(8,128)}, s32[8,128]{1,0:T(8,128)S(1)}, u32[]{:S(2)}, u32[]{:S(2)}) collective-permute-start(s32[8,128]{1,0:T(8,128)} %param.8), channel_id=1, source_target_pairs={{1,0},{2,1},{3,2},{4,3},{5,4},{6,5},{7,6},{8,7},{9,8},{10,9},{11,1... | collective-permute-start | bytes 12296 | tf_op jit(solution)/shard_map/ppermute | solution.py:25
  20.3 12.1 %collective-permute-start.13 = (f32[2,128]{1,0:T(2,128)S(1)}, f32[2,128]{1,0:T(2,128)S(1)}, u32[]{:S(2)}, u32[]{:S(2)}) collective-permute-start(f32[2,128]{1,0:T(2,128)S(1)} %get-tuple-element.173), channel_id=1, source_target_pairs={{1,0},{2,1},{3,2},{4,3},{5,4},{6,5},{7,6},{8,7},{9,8},{10,9},{11,1... | collective-permute-start | bytes 3080 | tf_op jit(solution)/shard_map/ppermute | solution.py:25
  80.5 18.2 %collective-permute-start.2 = (s32[24,8]{1,0:T(8,128)S(1)}, s32[24,8]{1,0:T(8,128)S(1)}, u32[]{:S(2)}, u32[]{:S(2)}) collective-permute-start(s32[24,8]{1,0:T(8,128)S(1)} %get-tuple-element.88), channel_id=1, source_target_pairs={{0,32},{32,64},{64,96},{96,128},{128,160},{160,192},{192,224},{224... | collective-permute-start | bytes 2312 | tf_op jit(solution)/shard_map/ppermute | solution.py:23
  100.7 14.5 %collective-permute-start.14 = (f32[12,2]{1,0:T(8,128)S(1)}, f32[12,2]{1,0:T(8,128)S(1)}, u32[]{:S(2)}, u32[]{:S(2)}) collective-permute-start(f32[12,2]{1,0:T(8,128)S(1)} %get-tuple-element.136), channel_id=1, source_target_pairs={{0,32},{32,64},{64,96},{96,128},{128,160},{160,192},{192,224},{224... | collective-permute-start | bytes 296 | tf_op jit(solution)/shard_map/ppermute | solution.py:23
  117.2 14.5 %collective-permute-start.10 = (f32[12,2]{1,0:T(8,128)S(1)}, f32[12,2]{1,0:T(8,128)S(1)}, u32[]{:S(2)}, u32[]{:S(2)}) collective-permute-start(f32[12,2]{1,0:T(8,128)S(1)} %get-tuple-element.134), channel_id=1, source_target_pairs={{0,32},{32,64},{64,96},{96,128},{128,160},{160,192},{192,224},{224... | collective-permute-start | bytes 296 | tf_op jit(solution)/shard_map/ppermute | solution.py:23
  133.7 14.5 %collective-permute-start.6 = (f32[12,2]{1,0:T(8,128)S(1)}, f32[12,2]{1,0:T(8,128)S(1)}, u32[]{:S(2)}, u32[]{:S(2)}) collective-permute-start(f32[12,2]{1,0:T(8,128)S(1)} %get-tuple-element.132), channel_id=1, source_target_pairs={{0,32},{32,64},{64,96},{96,128},{128,160},{160,192},{192,224},{224... | collective-permute-start | bytes 296 | tf_op jit(solution)/shard_map/ppermute | solution.py:23
  150.2 13.8 %collective-permute-done.7 = f32[12,2]{1,0:T(8,128)S(1)} collective-permute-done((f32[12,2]{1,0:T(8,128)S(1)}, f32[12,2]{1,0:T(8,128)S(1)}, u32[]{:S(2)}, u32[]{:S(2)}) %collective-permute-start.7) | collective-permute-done | bytes 128 | tf_op jit(solution)/shard_map/ppermute | solution.py:25
  166.5 12.4 %collective-permute-start.25 = (f32[2,128]{1,0:T(2,128)S(1)}, f32[2,128]{1,0:T(2,128)S(1)}, u32[]{:S(2)}, u32[]{:S(2)}) collective-permute-start(f32[2,128]{1,0:T(2,128)S(1)} %get-tuple-element.167), channel_id=1, source_target_pairs={{1,0},{2,1},{3,2},{4,3},{5,4},{6,5},{7,6},{8,7},{9,8},{10,9},{11,1... | collective-permute-start | bytes 3080 | tf_op jit(solution)/shard_map/ppermute | solution.py:25
  212.5 14.5 %collective-permute-start.22 = (f32[12,2]{1,0:T(8,128)S(1)}, f32[12,2]{1,0:T(8,128)S(1)}, u32[]{:S(2)}, u32[]{:S(2)}) collective-permute-start(f32[12,2]{1,0:T(8,128)S(1)} %get-tuple-element.128), channel_id=1, source_target_pairs={{0,32},{32,64},{64,96},{96,128},{128,160},{160,192},{192,224},{224... | collective-permute-start | bytes 296 | tf_op jit(solution)/shard_map/ppermute | solution.py:23
  229.0 14.5 %collective-permute-start.18 = (f32[12,2]{1,0:T(8,128)S(1)}, f32[12,2]{1,0:T(8,128)S(1)}, u32[]{:S(2)}, u32[]{:S(2)}) collective-permute-start(f32[12,2]{1,0:T(8,128)S(1)} %get-tuple-element.126), channel_id=1, source_target_pairs={{0,32},{32,64},{64,96},{96,128},{128,160},{160,192},{192,224},{224... | collective-permute-start | bytes 296 | tf_op jit(solution)/shard_map/ppermute | solution.py:23
  245.5 13.8 %collective-permute-done.19 = f32[12,2]{1,0:T(8,128)S(1)} collective-permute-done((f32[12,2]{1,0:T(8,128)S(1)}, f32[12,2]{1,0:T(8,128)S(1)}, u32[]{:S(2)}, u32[]{:S(2)}) %collective-permute-start.19) | collective-permute-done | bytes 128 | tf_op jit(solution)/shard_map/ppermute | solution.py:25
  307.4 14.5 %collective-permute-start.34 = (f32[12,2]{1,0:T(8,128)S(1)}, f32[12,2]{1,0:T(8,128)S(1)}, u32[]{:S(2)}, u32[]{:S(2)}) collective-permute-start(f32[12,2]{1,0:T(8,128)S(1)} %get-tuple-element.122), channel_id=1, source_target_pairs={{0,32},{32,64},{64,96},{96,128},{128,160},{160,192},{192,224},{224... | collective-permute-start | bytes 296 | tf_op jit(solution)/shard_map/ppermute | solution.py:23
  323.8 14.5 %collective-permute-start.30 = (f32[12,2]{1,0:T(8,128)S(1)}, f32[12,2]{1,0:T(8,128)S(1)}, u32[]{:S(2)}, u32[]{:S(2)}) collective-permute-start(f32[12,2]{1,0:T(8,128)S(1)} %get-tuple-element.120), channel_id=1, source_target_pairs={{0,32},{32,64},{64,96},{96,128},{128,160},{160,192},{192,224},{224... | collective-permute-start | bytes 296 | tf_op jit(solution)/shard_map/ppermute | solution.py:23
  340.3 13.8 %collective-permute-done.31 = f32[12,2]{1,0:T(8,128)S(1)} collective-permute-done((f32[12,2]{1,0:T(8,128)S(1)}, f32[12,2]{1,0:T(8,128)S(1)}, u32[]{:S(2)}, u32[]{:S(2)}) %collective-permute-start.31) | collective-permute-done | bytes 128 | tf_op jit(solution)/shard_map/ppermute | solution.py:25
  402.3 14.5 %collective-permute-start.46 = (f32[12,2]{1,0:T(8,128)S(1)}, f32[12,2]{1,0:T(8,128)S(1)}, u32[]{:S(2)}, u32[]{:S(2)}) collective-permute-start(f32[12,2]{1,0:T(8,128)S(1)} %get-tuple-element.116), channel_id=1, source_target_pairs={{0,32},{32,64},{64,96},{96,128},{128,160},{160,192},{192,224},{224... | collective-permute-start | bytes 296 | tf_op jit(solution)/shard_map/ppermute | solution.py:23
  418.7 14.5 %collective-permute-start.42 = (f32[12,2]{1,0:T(8,128)S(1)}, f32[12,2]{1,0:T(8,128)S(1)}, u32[]{:S(2)}, u32[]{:S(2)}) collective-permute-start(f32[12,2]{1,0:T(8,128)S(1)} %get-tuple-element.114), channel_id=1, source_target_pairs={{0,32},{32,64},{64,96},{96,128},{128,160},{160,192},{192,224},{224... | collective-permute-start | bytes 296 | tf_op jit(solution)/shard_map/ppermute | solution.py:23
  435.2 13.8 %collective-permute-done.43 = f32[12,2]{1,0:T(8,128)S(1)} collective-permute-done((f32[12,2]{1,0:T(8,128)S(1)}, f32[12,2]{1,0:T(8,128)S(1)}, u32[]{:S(2)}, u32[]{:S(2)}) %collective-permute-start.43) | collective-permute-done | bytes 128 | tf_op jit(solution)/shard_map/ppermute | solution.py:25
  497.1 14.5 %collective-permute-start.58 = (f32[12,2]{1,0:T(8,128)S(1)}, f32[12,2]{1,0:T(8,128)S(1)}, u32[]{:S(2)}, u32[]{:S(2)}) collective-permute-start(f32[12,2]{1,0:T(8,128)S(1)} %get-tuple-element.110), channel_id=1, source_target_pairs={{0,32},{32,64},{64,96},{96,128},{128,160},{160,192},{192,224},{224... | collective-permute-start | bytes 296 | tf_op jit(solution)/shard_map/ppermute | solution.py:23
  513.5 14.5 %collective-permute-start.54 = (f32[12,2]{1,0:T(8,128)S(1)}, f32[12,2]{1,0:T(8,128)S(1)}, u32[]{:S(2)}, u32[]{:S(2)}) collective-permute-start(f32[12,2]{1,0:T(8,128)S(1)} %get-tuple-element.108), channel_id=1, source_target_pairs={{0,32},{32,64},{64,96},{96,128},{128,160},{160,192},{192,224},{224... | collective-permute-start | bytes 296 | tf_op jit(solution)/shard_map/ppermute | solution.py:23
  530.1 13.8 %collective-permute-done.55 = f32[12,2]{1,0:T(8,128)S(1)} collective-permute-done((f32[12,2]{1,0:T(8,128)S(1)}, f32[12,2]{1,0:T(8,128)S(1)}, u32[]{:S(2)}, u32[]{:S(2)}) %collective-permute-start.55) | collective-permute-done | bytes 128 | tf_op jit(solution)/shard_map/ppermute | solution.py:25
  592.0 14.5 %collective-permute-start.70 = (f32[12,2]{1,0:T(8,128)S(1)}, f32[12,2]{1,0:T(8,128)S(1)}, u32[]{:S(2)}, u32[]{:S(2)}) collective-permute-start(f32[12,2]{1,0:T(8,128)S(1)} %get-tuple-element.104), channel_id=1, source_target_pairs={{0,32},{32,64},{64,96},{96,128},{128,160},{160,192},{192,224},{224... | collective-permute-start | bytes 296 | tf_op jit(solution)/shard_map/ppermute | solution.py:23
  608.4 14.5 %collective-permute-start.66 = (f32[12,2]{1,0:T(8,128)S(1)}, f32[12,2]{1,0:T(8,128)S(1)}, u32[]{:S(2)}, u32[]{:S(2)}) collective-permute-start(f32[12,2]{1,0:T(8,128)S(1)} %get-tuple-element.102), channel_id=1, source_target_pairs={{0,32},{32,64},{64,96},{96,128},{128,160},{160,192},{192,224},{224... | collective-permute-start | bytes 296 | tf_op jit(solution)/shard_map/ppermute | solution.py:23
  624.9 13.8 %collective-permute-done.67 = f32[12,2]{1,0:T(8,128)S(1)} collective-permute-done((f32[12,2]{1,0:T(8,128)S(1)}, f32[12,2]{1,0:T(8,128)S(1)}, u32[]{:S(2)}, u32[]{:S(2)}) %collective-permute-start.67) | collective-permute-done | bytes 128 | tf_op jit(solution)/shard_map/ppermute | solution.py:25
  686.9 14.5 %collective-permute-start.82 = (f32[12,2]{1,0:T(8,128)S(1)}, f32[12,2]{1,0:T(8,128)S(1)}, u32[]{:S(2)}, u32[]{:S(2)}) collective-permute-start(f32[12,2]{1,0:T(8,128)S(1)} %get-tuple-element.98), channel_id=1, source_target_pairs={{0,32},{32,64},{64,96},{96,128},{128,160},{160,192},{192,224},{224... | collective-permute-start | bytes 296 | tf_op jit(solution)/shard_map/ppermute | solution.py:23
  703.3 14.5 %collective-permute-start.78 = (f32[12,2]{1,0:T(8,128)S(1)}, f32[12,2]{1,0:T(8,128)S(1)}, u32[]{:S(2)}, u32[]{:S(2)}) collective-permute-start(f32[12,2]{1,0:T(8,128)S(1)} %get-tuple-element.96), channel_id=1, source_target_pairs={{0,32},{32,64},{64,96},{96,128},{128,160},{160,192},{192,224},{224... | collective-permute-start | bytes 296 | tf_op jit(solution)/shard_map/ppermute | solution.py:23
  719.8 13.8 %collective-permute-done.79 = f32[12,2]{1,0:T(8,128)S(1)} collective-permute-done((f32[12,2]{1,0:T(8,128)S(1)}, f32[12,2]{1,0:T(8,128)S(1)}, u32[]{:S(2)}, u32[]{:S(2)}) %collective-permute-start.79) | collective-permute-done | bytes 128 | tf_op jit(solution)/shard_map/ppermute | solution.py:25
  781.7 14.5 %collective-permute-start.94 = (f32[12,2]{1,0:T(8,128)S(1)}, f32[12,2]{1,0:T(8,128)S(1)}, u32[]{:S(2)}, u32[]{:S(2)}) collective-permute-start(f32[12,2]{1,0:T(8,128)S(1)} %get-tuple-element.92), channel_id=1, source_target_pairs={{0,32},{32,64},{64,96},{96,128},{128,160},{160,192},{192,224},{224... | collective-permute-start | bytes 296 | tf_op jit(solution)/shard_map/ppermute | solution.py:23
  798.1 14.5 %collective-permute-start.90 = (f32[12,2]{1,0:T(8,128)S(1)}, f32[12,2]{1,0:T(8,128)S(1)}, u32[]{:S(2)}, u32[]{:S(2)}) collective-permute-start(f32[12,2]{1,0:T(8,128)S(1)} %get-tuple-element.90), channel_id=1, source_target_pairs={{0,32},{32,64},{64,96},{96,128},{128,160},{160,192},{192,224},{224... | collective-permute-start | bytes 296 | tf_op jit(solution)/shard_map/ppermute | solution.py:23
  871.0 14.5 %collective-permute-start.110 = (f32[32,10,1]{2,1,0:T(8,128)S(1)}, f32[32,10,1]{2,1,0:T(8,128)S(1)}, u32[]{:S(2)}, u32[]{:S(2)}) collective-permute-start(f32[32,10,1]{2,1,0:T(8,128)S(1)} %get-tuple-element.17), channel_id=1, source_target_pairs={{0,32},{32,64},{64,96},{96,128},{128,160},{160,192},{192,224},{224... | collective-permute-start | bytes 3848 | tf_op jit(solution)/shard_map/ppermute | solution.py:23
  894.7 15.2 %collective-permute-start.115 = (f32[32,10,1]{2,1,0:T(8,128)S(1)}, f32[32,10,1]{2,1,0:T(8,128)S(1)}, u32[]{:S(2)}, u32[]{:S(2)}) collective-permute-start(f32[32,10,1]{2,1,0:T(8,128)S(1)} %get-tuple-element.14), channel_id=1, source_target_pairs={{0,32},{32,64},{64,96},{96,128},{128,160},{160,192},{192,224},{224... | collective-permute-start | bytes 3848 | tf_op jit(solution)/shard_map/ppermute | solution.py:23
  909.9 14.2 %collective-permute-done.107 = f32[32,10,1]{2,1,0:T(8,128)S(1)} collective-permute-done((f32[32,10,1]{2,1,0:T(8,128)S(1)}, f32[32,10,1]{2,1,0:T(8,128)S(1)}, u32[]{:S(2)}, u32[]{:S(2)}) %collective-permute-start.107) | collective-permute-done | bytes 1312 | tf_op jit(solution)/shard_map/ppermute | solution.py:25
  926.1 14.6 %collective-permute-start.103 = (f32[32,10,1]{2,1,0:T(8,128)S(1)}, f32[32,10,1]{2,1,0:T(8,128)S(1)}, u32[]{:S(2)}, u32[]{:S(2)}) collective-permute-start(f32[32,10,1]{2,1,0:T(8,128)S(1)} %get-tuple-element.16), channel_id=1, source_target_pairs={{0,32},{32,64},{64,96},{96,128},{128,160},{160,192},{192,224},{224... | collective-permute-start | bytes 3848 | tf_op jit(solution)/shard_map/ppermute | solution.py:23
  (347 shorter events, 486.3 us)
Async XLA Ops:
  0.6 79.1 %collective-permute-start = (s32[8,128]{1,0:T(8,128)}, s32[8,128]{1,0:T(8,128)S(1)}, u32[]{:S(2)}, u32[]{:S(2)}) collective-permute-start(s32[8,128]{1,0:T(8,128)} %param.8), channel_id=1, source_target_pairs={{0,1},{1,2},{2,3},{3,4},{4,5},{5,6},{6,7},{7,8},{8,9},{9,10},{10,1... | collective-permute-start | bytes 12296 | tf_op jit(solution)/shard_map/ppermute | solution.py:23
  4.2 76.3 %collective-permute-start.1 = (s32[8,128]{1,0:T(8,128)}, s32[8,128]{1,0:T(8,128)S(1)}, u32[]{:S(2)}, u32[]{:S(2)}) collective-permute-start(s32[8,128]{1,0:T(8,128)} %param.8), channel_id=1, source_target_pairs={{1,0},{2,1},{3,2},{4,3},{5,4},{6,5},{7,6},{8,7},{9,8},{10,9},{11,1... | collective-permute-start | bytes 12296 | tf_op jit(solution)/shard_map/ppermute | solution.py:25
  18.4 19.1 %collective-permute-start.12 = (f32[2,128]{1,0:T(2,128)S(1)}, f32[2,128]{1,0:T(2,128)S(1)}, u32[]{:S(2)}, u32[]{:S(2)}) collective-permute-start(f32[2,128]{1,0:T(2,128)S(1)} %get-tuple-element.172), channel_id=1, source_target_pairs={{0,1},{1,2},{2,3},{3,4},{4,5},{5,6},{6,7},{7,8},{8,9},{9,10},{10,1... | collective-permute-start | bytes 3080 | tf_op jit(solution)/shard_map/ppermute | solution.py:23
  20.3 29.3 %collective-permute-start.13 = (f32[2,128]{1,0:T(2,128)S(1)}, f32[2,128]{1,0:T(2,128)S(1)}, u32[]{:S(2)}, u32[]{:S(2)}) collective-permute-start(f32[2,128]{1,0:T(2,128)S(1)} %get-tuple-element.173), channel_id=1, source_target_pairs={{1,0},{2,1},{3,2},{4,3},{5,4},{6,5},{7,6},{8,7},{9,8},{10,9},{11,1... | collective-permute-start | bytes 3080 | tf_op jit(solution)/shard_map/ppermute | solution.py:25
  32.4 19.2 %collective-permute-start.8 = (f32[2,128]{1,0:T(2,128)S(1)}, f32[2,128]{1,0:T(2,128)S(1)}, u32[]{:S(2)}, u32[]{:S(2)}) collective-permute-start(f32[2,128]{1,0:T(2,128)S(1)} %get-tuple-element.170), channel_id=1, source_target_pairs={{0,1},{1,2},{2,3},{3,4},{4,5},{5,6},{6,7},{7,8},{8,9},{9,10},{10,1... | collective-permute-start | bytes 3080 | tf_op jit(solution)/shard_map/ppermute | solution.py:23
  37.5 26.2 %collective-permute-start.9 = (f32[2,128]{1,0:T(2,128)S(1)}, f32[2,128]{1,0:T(2,128)S(1)}, u32[]{:S(2)}, u32[]{:S(2)}) collective-permute-start(f32[2,128]{1,0:T(2,128)S(1)} %get-tuple-element.171), channel_id=1, source_target_pairs={{1,0},{2,1},{3,2},{4,3},{5,4},{6,5},{7,6},{8,7},{9,8},{10,9},{11,1... | collective-permute-start | bytes 3080 | tf_op jit(solution)/shard_map/ppermute | solution.py:25
  51.6 26.2 %collective-permute-start.5 = (f32[2,128]{1,0:T(2,128)S(1)}, f32[2,128]{1,0:T(2,128)S(1)}, u32[]{:S(2)}, u32[]{:S(2)}) collective-permute-start(f32[2,128]{1,0:T(2,128)S(1)} %get-tuple-element.169), channel_id=1, source_target_pairs={{1,0},{2,1},{3,2},{4,3},{5,4},{6,5},{7,6},{8,7},{9,8},{10,9},{11,1... | collective-permute-start | bytes 3080 | tf_op jit(solution)/shard_map/ppermute | solution.py:25
  63.7 767.4 %collective-permute-start.104 = (f32[32,1,128]{2,1,0:T(1,128)S(1)}, f32[32,1,128]{2,1,0:T(1,128)S(1)}, u32[]{:S(2)}, u32[]{:S(2)}) collective-permute-start(f32[32,1,128]{2,1,0:T(1,128)S(1)} %get-tuple-element.31), channel_id=1, source_target_pairs={{0,1},{1,2},{2,3},{3,4},{4,5},{5,6},{6,7},{7,8},{8,9},{9,10},{10,1... | collective-permute-start | bytes 49160 | tf_op jit(solution)/shard_map/ppermute | solution.py:23
  65.7 777.5 %collective-permute-start.105 = (f32[32,1,128]{2,1,0:T(1,128)S(1)}, f32[32,1,128]{2,1,0:T(1,128)S(1)}, u32[]{:S(2)}, u32[]{:S(2)}) collective-permute-start(f32[32,1,128]{2,1,0:T(1,128)S(1)} %get-tuple-element.32), channel_id=1, source_target_pairs={{1,0},{2,1},{3,2},{4,3},{5,4},{6,5},{7,6},{8,7},{9,8},{10,9},{11,1... | collective-permute-start | bytes 49160 | tf_op jit(solution)/shard_map/ppermute | solution.py:25
  77.8 767.5 %collective-permute-start.108 = (f32[32,1,128]{2,1,0:T(1,128)S(1)}, f32[32,1,128]{2,1,0:T(1,128)S(1)}, u32[]{:S(2)}, u32[]{:S(2)}) collective-permute-start(f32[32,1,128]{2,1,0:T(1,128)S(1)} %get-tuple-element.29), channel_id=1, source_target_pairs={{0,1},{1,2},{2,3},{3,4},{4,5},{5,6},{6,7},{7,8},{8,9},{9,10},{10,1... | collective-permute-start | bytes 49160 | tf_op jit(solution)/shard_map/ppermute | solution.py:23
  80.5 20.2 %collective-permute-start.2 = (s32[24,8]{1,0:T(8,128)S(1)}, s32[24,8]{1,0:T(8,128)S(1)}, u32[]{:S(2)}, u32[]{:S(2)}) collective-permute-start(s32[24,8]{1,0:T(8,128)S(1)} %get-tuple-element.88), channel_id=1, source_target_pairs={{0,32},{32,64},{64,96},{96,128},{128,160},{160,192},{192,224},{224... | collective-permute-start | bytes 2312 | tf_op jit(solution)/shard_map/ppermute | solution.py:23
  115.2 16.5 %collective-permute-start.15 = (f32[12,2]{1,0:T(8,128)S(1)}, f32[12,2]{1,0:T(8,128)S(1)}, u32[]{:S(2)}, u32[]{:S(2)}) collective-permute-start(f32[12,2]{1,0:T(8,128)S(1)} %get-tuple-element.137), channel_id=1, source_target_pairs={{32,0},{64,32},{96,64},{128,96},{160,128},{192,160},{224,192},{256... | collective-permute-start | bytes 296 | tf_op jit(solution)/shard_map/ppermute | solution.py:25
  133.7 16.5 %collective-permute-start.6 = (f32[12,2]{1,0:T(8,128)S(1)}, f32[12,2]{1,0:T(8,128)S(1)}, u32[]{:S(2)}, u32[]{:S(2)}) collective-permute-start(f32[12,2]{1,0:T(8,128)S(1)} %get-tuple-element.132), channel_id=1, source_target_pairs={{0,32},{32,64},{64,96},{96,128},{128,160},{160,192},{192,224},{224... | collective-permute-start | bytes 296 | tf_op jit(solution)/shard_map/ppermute | solution.py:23
  229.0 16.5 %collective-permute-start.18 = (f32[12,2]{1,0:T(8,128)S(1)}, f32[12,2]{1,0:T(8,128)S(1)}, u32[]{:S(2)}, u32[]{:S(2)}) collective-permute-start(f32[12,2]{1,0:T(8,128)S(1)} %get-tuple-element.126), channel_id=1, source_target_pairs={{0,32},{32,64},{64,96},{96,128},{128,160},{160,192},{192,224},{224... | collective-permute-start | bytes 296 | tf_op jit(solution)/shard_map/ppermute | solution.py:23
  323.8 16.5 %collective-permute-start.30 = (f32[12,2]{1,0:T(8,128)S(1)}, f32[12,2]{1,0:T(8,128)S(1)}, u32[]{:S(2)}, u32[]{:S(2)}) collective-permute-start(f32[12,2]{1,0:T(8,128)S(1)} %get-tuple-element.120), channel_id=1, source_target_pairs={{0,32},{32,64},{64,96},{96,128},{128,160},{160,192},{192,224},{224... | collective-permute-start | bytes 296 | tf_op jit(solution)/shard_map/ppermute | solution.py:23
  418.7 16.5 %collective-permute-start.42 = (f32[12,2]{1,0:T(8,128)S(1)}, f32[12,2]{1,0:T(8,128)S(1)}, u32[]{:S(2)}, u32[]{:S(2)}) collective-permute-start(f32[12,2]{1,0:T(8,128)S(1)} %get-tuple-element.114), channel_id=1, source_target_pairs={{0,32},{32,64},{64,96},{96,128},{128,160},{160,192},{192,224},{224... | collective-permute-start | bytes 296 | tf_op jit(solution)/shard_map/ppermute | solution.py:23
  513.5 16.5 %collective-permute-start.54 = (f32[12,2]{1,0:T(8,128)S(1)}, f32[12,2]{1,0:T(8,128)S(1)}, u32[]{:S(2)}, u32[]{:S(2)}) collective-permute-start(f32[12,2]{1,0:T(8,128)S(1)} %get-tuple-element.108), channel_id=1, source_target_pairs={{0,32},{32,64},{64,96},{96,128},{128,160},{160,192},{192,224},{224... | collective-permute-start | bytes 296 | tf_op jit(solution)/shard_map/ppermute | solution.py:23
  608.4 16.5 %collective-permute-start.66 = (f32[12,2]{1,0:T(8,128)S(1)}, f32[12,2]{1,0:T(8,128)S(1)}, u32[]{:S(2)}, u32[]{:S(2)}) collective-permute-start(f32[12,2]{1,0:T(8,128)S(1)} %get-tuple-element.102), channel_id=1, source_target_pairs={{0,32},{32,64},{64,96},{96,128},{128,160},{160,192},{192,224},{224... | collective-permute-start | bytes 296 | tf_op jit(solution)/shard_map/ppermute | solution.py:23
  703.3 16.5 %collective-permute-start.78 = (f32[12,2]{1,0:T(8,128)S(1)}, f32[12,2]{1,0:T(8,128)S(1)}, u32[]{:S(2)}, u32[]{:S(2)}) collective-permute-start(f32[12,2]{1,0:T(8,128)S(1)} %get-tuple-element.96), channel_id=1, source_target_pairs={{0,32},{32,64},{64,96},{96,128},{128,160},{160,192},{192,224},{224... | collective-permute-start | bytes 296 | tf_op jit(solution)/shard_map/ppermute | solution.py:23
  814.7 42.8 %collective-permute-start.109 = (f32[32,1,128]{2,1,0:T(1,128)S(1)}, f32[32,1,128]{2,1,0:T(1,128)S(1)}, u32[]{:S(2)}, u32[]{:S(2)}) collective-permute-start(f32[32,1,128]{2,1,0:T(1,128)S(1)} %get-tuple-element.30), channel_id=1, source_target_pairs={{1,0},{2,1},{3,2},{4,3},{5,4},{6,5},{7,6},{8,7},{9,8},{10,9},{11,1... | collective-permute-start | bytes 49160 | tf_op jit(solution)/shard_map/ppermute | solution.py:25
  828.4 40.7 %collective-permute-start.112 = (f32[32,1,128]{2,1,0:T(1,128)S(1)}, f32[32,1,128]{2,1,0:T(1,128)S(1)}, u32[]{:S(2)}, u32[]{:S(2)}) collective-permute-start(f32[32,1,128]{2,1,0:T(1,128)S(1)} %get-tuple-element.26), channel_id=1, source_target_pairs={{0,1},{1,2},{2,3},{3,4},{4,5},{5,6},{6,7},{7,8},{8,9},{9,10},{10,1... | collective-permute-start | bytes 49160 | tf_op jit(solution)/shard_map/ppermute | solution.py:23
  831.1 39.9 %collective-permute-start.113 = (f32[32,1,128]{2,1,0:T(1,128)S(1)}, f32[32,1,128]{2,1,0:T(1,128)S(1)}, u32[]{:S(2)}, u32[]{:S(2)}) collective-permute-start(f32[32,1,128]{2,1,0:T(1,128)S(1)} %get-tuple-element.25), channel_id=1, source_target_pairs={{1,0},{2,1},{3,2},{4,3},{5,4},{6,5},{7,6},{8,7},{9,8},{10,9},{11,1... | collective-permute-start | bytes 49160 | tf_op jit(solution)/shard_map/ppermute | solution.py:25
  843.2 42.5 %collective-permute-start.100 = (f32[32,1,128]{2,1,0:T(1,128)S(1)}, f32[32,1,128]{2,1,0:T(1,128)S(1)}, u32[]{:S(2)}, u32[]{:S(2)}) collective-permute-start(f32[32,1,128]{2,1,0:T(1,128)S(1)} %get-tuple-element.28), channel_id=1, source_target_pairs={{0,1},{1,2},{2,3},{3,4},{4,5},{5,6},{6,7},{7,8},{8,9},{9,10},{10,1... | collective-permute-start | bytes 49160 | tf_op jit(solution)/shard_map/ppermute | solution.py:23
  845.3 42.3 %collective-permute-start.101 = (f32[32,1,128]{2,1,0:T(1,128)S(1)}, f32[32,1,128]{2,1,0:T(1,128)S(1)}, u32[]{:S(2)}, u32[]{:S(2)}) collective-permute-start(f32[32,1,128]{2,1,0:T(1,128)S(1)} %get-tuple-element.27), channel_id=1, source_target_pairs={{1,0},{2,1},{3,2},{4,3},{5,4},{6,5},{7,6},{8,7},{9,8},{10,9},{11,1... | collective-permute-start | bytes 49160 | tf_op jit(solution)/shard_map/ppermute | solution.py:25
  857.4 37.2 %collective-permute-start.106 = (f32[32,10,1]{2,1,0:T(8,128)S(1)}, f32[32,10,1]{2,1,0:T(8,128)S(1)}, u32[]{:S(2)}, u32[]{:S(2)}) collective-permute-start(f32[32,10,1]{2,1,0:T(8,128)S(1)} %get-tuple-element.19), channel_id=1, source_target_pairs={{0,32},{32,64},{64,96},{96,128},{128,160},{160,192},{192,224},{224... | collective-permute-start | bytes 3848 | tf_op jit(solution)/shard_map/ppermute | solution.py:23
  869.1 55.0 %collective-permute-start.107 = (f32[32,10,1]{2,1,0:T(8,128)S(1)}, f32[32,10,1]{2,1,0:T(8,128)S(1)}, u32[]{:S(2)}, u32[]{:S(2)}) collective-permute-start(f32[32,10,1]{2,1,0:T(8,128)S(1)} %get-tuple-element.20), channel_id=1, source_target_pairs={{32,0},{64,32},{96,64},{128,96},{160,128},{192,160},{224,192},{256... | collective-permute-start | bytes 3848 | tf_op jit(solution)/shard_map/ppermute | solution.py:25
  871.0 55.0 %collective-permute-start.110 = (f32[32,10,1]{2,1,0:T(8,128)S(1)}, f32[32,10,1]{2,1,0:T(8,128)S(1)}, u32[]{:S(2)}, u32[]{:S(2)}) collective-permute-start(f32[32,10,1]{2,1,0:T(8,128)S(1)} %get-tuple-element.17), channel_id=1, source_target_pairs={{0,32},{32,64},{64,96},{96,128},{128,160},{160,192},{192,224},{224... | collective-permute-start | bytes 3848 | tf_op jit(solution)/shard_map/ppermute | solution.py:23
  885.7 55.0 %collective-permute-start.111 = (f32[32,10,1]{2,1,0:T(8,128)S(1)}, f32[32,10,1]{2,1,0:T(8,128)S(1)}, u32[]{:S(2)}, u32[]{:S(2)}) collective-permute-start(f32[32,10,1]{2,1,0:T(8,128)S(1)} %get-tuple-element.18), channel_id=1, source_target_pairs={{32,0},{64,32},{96,64},{128,96},{160,128},{192,160},{224,192},{256... | collective-permute-start | bytes 3848 | tf_op jit(solution)/shard_map/ppermute | solution.py:25
  887.6 54.9 %collective-permute-start.114 = (f32[32,10,1]{2,1,0:T(8,128)S(1)}, f32[32,10,1]{2,1,0:T(8,128)S(1)}, u32[]{:S(2)}, u32[]{:S(2)}) collective-permute-start(f32[32,10,1]{2,1,0:T(8,128)S(1)} %get-tuple-element.13), channel_id=1, source_target_pairs={{32,0},{64,32},{96,64},{128,96},{160,128},{192,160},{224,192},{256... | collective-permute-start | bytes 3848 | tf_op jit(solution)/shard_map/ppermute | solution.py:25
  894.7 47.9 %collective-permute-start.115 = (f32[32,10,1]{2,1,0:T(8,128)S(1)}, f32[32,10,1]{2,1,0:T(8,128)S(1)}, u32[]{:S(2)}, u32[]{:S(2)}) collective-permute-start(f32[32,10,1]{2,1,0:T(8,128)S(1)} %get-tuple-element.14), channel_id=1, source_target_pairs={{0,32},{32,64},{64,96},{96,128},{128,160},{160,192},{192,224},{224... | collective-permute-start | bytes 3848 | tf_op jit(solution)/shard_map/ppermute | solution.py:23
  924.1 20.6 %collective-permute-start.102 = (f32[32,10,1]{2,1,0:T(8,128)S(1)}, f32[32,10,1]{2,1,0:T(8,128)S(1)}, u32[]{:S(2)}, u32[]{:S(2)}) collective-permute-start(f32[32,10,1]{2,1,0:T(8,128)S(1)} %get-tuple-element.15), channel_id=1, source_target_pairs={{32,0},{64,32},{96,64},{128,96},{160,128},{192,160},{224,192},{256... | collective-permute-start | bytes 3848 | tf_op jit(solution)/shard_map/ppermute | solution.py:25
  926.1 18.7 %collective-permute-start.103 = (f32[32,10,1]{2,1,0:T(8,128)S(1)}, f32[32,10,1]{2,1,0:T(8,128)S(1)}, u32[]{:S(2)}, u32[]{:S(2)}) collective-permute-start(f32[32,10,1]{2,1,0:T(8,128)S(1)} %get-tuple-element.16), channel_id=1, source_target_pairs={{0,32},{32,64},{64,96},{96,128},{128,160},{160,192},{192,224},{224... | collective-permute-start | bytes 3848 | tf_op jit(solution)/shard_map/ppermute | solution.py:23
  (94 other events, 1511.8 us)
where the time goes:
time: 950 us; the launch traced here: 946 us
  starting transfers between devices  807 us (85%)
  waiting for transfers between devices  120 us (13%)
    ppermute x58, starting transfers between devices, extended(): lax.ppermute(head, axis, [((i + 1) % count, i) for i in range(count)])  405 us
    ppermute x58, starting transfers between devices, extended(): lax.ppermute(tail, axis, [(i, (i + 1) % count) for i in range(count)])  402 us
    ppermute x58, waiting for transfers between devices, extended(): lax.ppermute(head, axis, [((i + 1) % count, i) for i in range(count)])  115 us
  transfers between devices with their start and end apart: 116, of which 10 were waited for; matrix products, arithmetic and copies ran while one was open for 1% of the time, Pallas kernels for 0%

commit v1 on v0

v1 whole, which is shorter than its diff:
```python
import functools

import jax
import jax.numpy as jnp
from jax import lax
from jax.experimental import pallas as pl
from jax.experimental.pallas import tpu as pltpu
from jax.sharding import PartitionSpec as P

LEVELS = 32
SUBCYCLES = 8
ROWS = 8
COLS = 128
EDGE = 16
WAVE = 0.45
CORIOLIS = 0.12
DIAPYCNAL = 0.2
UNROLL = 4

SIDES = [(a, o) for o in (-1, 1) for a in (-2, -1, 0, 1, 2)]
STACKS = [(a, 0) for a in (-2, -1, 1, 2)]
OFFSETS = SIDES + STACKS
f32 = jnp.float32


def kernel(
    bottom_hbm, level_hbm, flow_x_hbm, flow_y_hbm, x_hbm, y_hbm, t_hbm, s_hbm,
    level_out, east_out, north_out, x_out, y_out, t_out, s_out,
    bottom, own, big, edge, side_recv, stack_recv,
    row_first, row_last, row_north, row_south,
    col_to_east, col_to_west, col_from_west, col_from_east,
    local_sem, send_sem, recv_sem,
):
    lat, lon = lax.axis_index("lat"), lax.axis_index("lon")
    lats, lons = lax.axis_size("lat"), lax.axis_size("lon")

    def place(offset):
        return {
            "lat": lax.rem(lat + offset[0] + lats, lats),
            "lon": lax.rem(lon + offset[1] + lons, lons),
        }

    barrier = pltpu.get_barrier_semaphore()
    for offset in OFFSETS:
        pl.semaphore_signal(
            barrier, inc=1, device_id=place(offset), device_id_type=pl.DeviceIdType.MESH
        )

    small = [
        pltpu.make_async_copy(bottom_hbm, bottom, local_sem.at[0]),
        pltpu.make_async_copy(level_hbm, own.at[1], local_sem.at[1]),
        pltpu.make_async_copy(flow_x_hbm, own.at[2], local_sem.at[2]),
        pltpu.make_async_copy(flow_y_hbm, own.at[3], local_sem.at[3]),
    ]
    large = [
        pltpu.make_async_copy(ref, big.at[i], local_sem.at[4 + i])
        for i, ref in enumerate((x_hbm, y_hbm, t_hbm, s_hbm))
    ]
    for copy in small + large:
        copy.start()

    lane = lax.broadcasted_iota(jnp.int32, (ROWS, COLS), 1)
    row = lax.broadcasted_iota(jnp.int32, (ROWS, COLS), 0)
    even = lane % 2 == 0

    def roll(cells, shift):
        return pltpu.roll(cells, shift % COLS, 1)

    def slide(cells, shift):
        return pltpu.roll(cells, shift % ROWS, 0)

    for copy in small:
        copy.wait()
    own[0] = bottom[...].astype(f32)
    packed = roll(own[0], EDGE)
    for i in range(1, 4):
        packed = jnp.where(lane // 32 == i, roll(own[i], EDGE + 32 * i), packed)
    edge[...] = packed

    for copy in large:
        copy.wait()
    for i in range(4):
        row_first[pl.ds(i * LEVELS, LEVELS), :] = big[i, :, 0, :]
        row_last[pl.ds(i * LEVELS, LEVELS), :] = big[i, :, ROWS - 1, :]

    def pack(k, carry):
        first, second = carry
        first = jnp.where(lane // 2 == k, pltpu.roll(big[0, k], 2 * k + 1, 1), first)
        first = jnp.where(lane // 2 == k + 32, pltpu.roll(big[1, k], 2 * k + 65, 1), first)
        second = jnp.where(lane // 2 == k, pltpu.roll(big[2, k], 2 * k + 1, 1), second)
        second = jnp.where(
            lane // 2 == k + 32, pltpu.roll(big[3, k], (2 * k + 65) % COLS, 1), second
        )
        return first, second

    zero = jnp.zeros((ROWS, COLS), f32)
    first, second = lax.fori_loop(0, LEVELS, pack, (zero, zero), unroll=LEVELS)
    col_to_east[...] = jnp.where(even, first, roll(second, 1))
    col_to_west[...] = jnp.where(even, roll(first, -1), second)

    pl.semaphore_wait(barrier, len(OFFSETS))

    copies = []

    def send(src, dst, index, offset):
        copy = pltpu.make_async_remote_copy(
            src_ref=src,
            dst_ref=dst,
            send_sem=send_sem.at[index],
            recv_sem=recv_sem.at[index],
            device_id=place(offset),
            device_id_type=pl.DeviceIdType.MESH,
        )
        copy.start()
        copies.append(copy)

    for a, o in SIDES:
        slot = SIDES.index((-a, -o))
        send(edge, side_recv.at[slot], slot, (a, o))
    for a, o in STACKS:
        slot = STACKS.index((-a, -o))
        send(own, stack_recv.at[slot], len(SIDES) + slot, (a, o))
    halo_count = len(OFFSETS)
    send(col_to_east, col_from_west, halo_count, (0, 1))
    send(col_to_west, col_from_east, halo_count + 1, (0, -1))
    send(row_last, row_south, halo_count + 2, (1, 0))
    send(row_first, row_north, halo_count + 3, (-1, 0))

    centre = own[0]
    coef = 0.08 + (0.12 / LEVELS) * centre
    bottom_e = jnp.where(lane == COLS - 1, 0.0, roll(centre, -1))
    bottom_w = jnp.where(lane == 0, 0.0, roll(centre, 1))
    bottom_n = jnp.where(row == ROWS - 1, 0.0, slide(centre, -1))
    bottom_s = jnp.where(row == 0, 0.0, slide(centre, 1))

    def inner(k, carry):
        press, sum_x, sum_y = carry
        depth = lax.convert_element_type(k, f32)
        wet = centre > depth
        wet_e, wet_w = bottom_e > depth, bottom_w > depth
        wet_n, wet_s = bottom_n > depth, bottom_s > depth

        def lateral(cells):
            return (
                jnp.where(wet_e, roll(cells, -1), cells)
                + jnp.where(wet_w, roll(cells, 1), cells)
                + jnp.where(wet_n, slide(cells, -1), cells)
                + jnp.where(wet_s, slide(cells, 1), cells)
                - 4.0 * cells
            )

        x, y, t, s = big[0, k], big[1, k], big[2, k], big[3, k]
        press = press + jnp.where(wet, 0.6 * s - 0.8 * t, 0.0)
        press_x = jnp.where(lane == COLS - 1, 0.0, roll(press, -1)) - jnp.where(
            lane == 0, 0.0, roll(press, 1)
        )
        press_y = jnp.where(row == ROWS - 1, 0.0, slide(press, -1)) - jnp.where(
            row == 0, 0.0, slide(press, 1)
        )
        x_out[k] = x + coef * lateral(x) + CORIOLIS * y - 0.1 * press_x
        y_out[k] = y + coef * lateral(y) - CORIOLIS * x - 0.1 * press_y
        below = centre > depth + 1.0
        up, down = lax.max(k - 1, 0), lax.min(k + 1, LEVELS - 1)
        for i, cells, out in ((2, t, t_out), (3, s, s_out)):
            vertical = (big[i, up] - cells) + jnp.where(below, big[i, down] - cells, 0.0)
            out[k] = cells + coef * lateral(cells) + DIAPYCNAL * vertical
        return press, sum_x + jnp.where(wet, x, 0.0), sum_y + jnp.where(wet, y, 0.0)

    _, sum_x, sum_y = lax.fori_loop(0, LEVELS, inner, (zero, zero, zero), unroll=UNROLL)
    count = jnp.maximum(centre, 1.0)
    mean_x, mean_y = sum_x / count, sum_y / count

    for copy in copies[:halo_count]:
        copy.wait_recv()

    fields = [[], [], [], []]
    for a in (-2, -1, 0, 1, 2):
        inside = (lat + a >= 0) & (lat + a < lats)
        keep = jnp.where(inside, 1.0, 0.0).astype(f32)
        merged = jnp.where(
            lane % 32 < EDGE, side_recv[SIDES.index((a, -1))], side_recv[SIDES.index((a, 1))]
        )
        for i in range(4):
            middle = own[i] if a == 0 else stack_recv[STACKS.index((a, 0)), i]
            beside = roll(merged, -(EDGE + 32 * i))
            if i == 0 and a != 0:
                middle, beside = middle * keep, beside * keep
            fields[i].append((middle, beside))
    halo_bottom = fields[0]

    def whole(tiles):
        return jnp.concatenate(
            [jnp.concatenate([m for m, _ in tiles], 0), jnp.concatenate([b for _, b in tiles], 0)], 1
        )

    def ew(cells):
        return pltpu.roll(cells, 2 * COLS - 1, 1) - pltpu.roll(cells, 1, 1)

    def ns(cells):
        return pltpu.roll(cells, cells.shape[0] - 1, 0) - pltpu.roll(cells, 1, 0)

    column, level, flow_x, flow_y = (whole(tiles) for tiles in fields)
    wet = jnp.where(column > 0.0, 1.0, 0.0)
    gain = (WAVE / LEVELS) * column
    level, flow_x, flow_y = wet * level, wet * flow_x, wet * flow_y
    for cycle in range(SUBCYCLES):
        level = level - wet * (ew(gain * flow_x) + ns(gain * flow_y))
        flow_x, flow_y = (
            flow_x - gain * ew(level) + CORIOLIS * flow_y,
            flow_y - gain * ns(level) - CORIOLIS * flow_x,
        )
        if cycle == 3:
            wet, gain, level, flow_x, flow_y = (
                cells[ROWS : 4 * ROWS] for cells in (wet, gain, level, flow_x, flow_y)
            )
    level, flow_x, flow_y = (cells[ROWS : 2 * ROWS, :COLS] for cells in (level, flow_x, flow_y))
    level_out[...] = level
    east_out[...] = flow_x
    north_out[...] = flow_y

    for copy in copies[halo_count:]:
        copy.wait_recv()

    beside = halo_bottom[2][1]
    bottom_ew = jnp.where(
        lane == COLS - 1, roll(beside, -1), jnp.where(lane == 0, roll(beside, 1), 0.0)
    )
    bottom_ns = jnp.where(
        row == ROWS - 1,
        slide(halo_bottom[3][0], -1),
        jnp.where(row == 0, slide(halo_bottom[1][0], 1), 0.0),
    )
    from_east, from_west = col_from_east[...], col_from_west[...]
    first = jnp.where(even, from_east, roll(from_west, 1))
    second = jnp.where(even, roll(from_east, -1), from_west)
    sign_ew = jnp.where(lane == COLS - 1, 1.0, -1.0)
    sign_ns = jnp.where(row == ROWS - 1, 1.0, -1.0)
    t_ew, s_ew = 0.08 * sign_ew, -0.06 * sign_ew
    t_ns, s_ns = 0.08 * sign_ns, -0.06 * sign_ns
    add_x, add_y = flow_x - mean_x, flow_y - mean_y
    upper = row < ROWS // 2

    def outer(k, carry):
        press_ew, press_ns = carry
        depth = lax.convert_element_type(k, f32)
        wet = centre > depth
        wet_ew, wet_ns = bottom_ew > depth, bottom_ns > depth
        sides = [
            pltpu.roll(source, (COLS - 1 - 2 * (k + base)) % COLS, 1)
            for source, base in ((first, 0), (first, 32), (second, 0), (second, 32))
        ]
        stacks = [
            jnp.where(
                upper,
                jnp.broadcast_to(row_south[pl.ds(i * LEVELS + k, 1), :], (ROWS, COLS)),
                jnp.broadcast_to(row_north[pl.ds(i * LEVELS + k, 1), :], (ROWS, COLS)),
            )
            for i in range(4)
        ]

        def lateral(i):
            cells = big[i, k]
            return jnp.where(wet_ew, sides[i] - cells, 0.0) + jnp.where(
                wet_ns, stacks[i] - cells, 0.0
            )

        press_ew = press_ew + jnp.where(wet_ew, t_ew * sides[2] + s_ew * sides[3], 0.0)
        press_ns = press_ns + jnp.where(wet_ns, t_ns * stacks[2] + s_ns * stacks[3], 0.0)
        x_out[k] = jnp.where(wet, x_out[k] + coef * lateral(0) + (press_ew + add_x), 0.0)
        y_out[k] = jnp.where(wet, y_out[k] + coef * lateral(1) + (press_ns + add_y), 0.0)
        t_out[k] = jnp.where(wet, t_out[k] + coef * lateral(2), 0.0)
        s_out[k] = jnp.where(wet, s_out[k] + coef * lateral(3), 0.0)
        return press_ew, press_ns

    lax.fori_loop(0, LEVELS, outer, (zero, zero), unroll=UNROLL)

    for copy in copies:
        copy.wait_send()


def body(*args):
    flat = jax.ShapeDtypeStruct((ROWS, COLS), f32)
    deep = jax.ShapeDtypeStruct((LEVELS, ROWS, COLS), f32)
    messages = len(OFFSETS) + 4
    return pl.pallas_call(
        kernel,
        out_shape=(flat,) * 3 + (deep,) * 4,
        in_specs=[pl.BlockSpec(memory_space=pl.ANY)] * 8,
        out_specs=(pl.BlockSpec(memory_space=pltpu.VMEM),) * 7,
        scratch_shapes=[
            pltpu.VMEM((ROWS, COLS), jnp.int32),
            pltpu.VMEM((4, ROWS, COLS), f32),
            pltpu.VMEM((4, LEVELS, ROWS, COLS), f32),
            pltpu.VMEM((ROWS, COLS), f32),
            pltpu.VMEM((len(SIDES), ROWS, COLS), f32),
            pltpu.VMEM((len(STACKS), 4, ROWS, COLS), f32),
            pltpu.VMEM((4 * LEVELS, COLS), f32),
            pltpu.VMEM((4 * LEVELS, COLS), f32),
            pltpu.VMEM((4 * LEVELS, COLS), f32),
            pltpu.VMEM((4 * LEVELS, COLS), f32),
            pltpu.VMEM((ROWS, COLS), f32),
            pltpu.VMEM((ROWS, COLS), f32),
            pltpu.VMEM((ROWS, COLS), f32),
            pltpu.VMEM((ROWS, COLS), f32),
            pltpu.SemaphoreType.DMA((8,)),
            pltpu.SemaphoreType.DMA((messages,)),
            pltpu.SemaphoreType.DMA((messages,)),
        ],
        compiler_params=pltpu.CompilerParams(
            collective_id=0, has_side_effects=True, vmem_limit_bytes=16 * 1024 * 1024
        ),
    )(*args)


def solution(mesh):
    flat, deep = P("lat", "lon"), P(None, "lat", "lon")
    return jax.shard_map(
        body,
        mesh=mesh,
        in_specs=(flat,) * 4 + (deep,) * 4,
        out_specs=(flat,) * 3 + (deep,) * 4,
        check_vma=False,
    )
```

time: 950 us -> 51.1 us (0.05)
  the two profiles are of different devices: /device:TPU:25 before, /device:TPU:1 now
where the time goes in v1:
time: 51.1 us; the launch traced here: 50.7 us
  Pallas kernels  39.3 us (77%)
  local copies, waits for them, and re-layouts  10.8 us (21%)
  between operations  0.66 us (1%)
    pallas_call x1, Pallas kernels, body(): pl.pallas_call(kernel, out_shape=(flat,) * 3 + (deep,) * 4, in_specs=[pl....  39.3 us
    unnamed x23, local copies, waits for them, and re-layouts  10.8 us

profile of v1, /device:TPU:1, one launch (start us, length us, event | category | flops | bytes accessed | tf_op | source)
XLA Modules:
  0.0 50.7 jit_solution(9579968198546781178)
XLA Ops:
  0.6 0.0 copy-start
  0.6 0.9 %copy-done = f32[32,8,128]{2,1,0:T(8,128)S(1)} copy-done((f32[32,8,128]{2,1,0:T(8,128)S(1)}, f32[32,8,128]{2,1,0:T(8,128)}, u32[]{:S(2)}) %copy-start) | copy-done | bytes 131096
  1.5 0.0 copy-start.1
  1.5 0.9 %copy-done.1 = f32[32,8,128]{2,1,0:T(8,128)S(1)} copy-done((f32[32,8,128]{2,1,0:T(8,128)S(1)}, f32[32,8,128]{2,1,0:T(8,128)}, u32[]{:S(2)}) %copy-start.1) | copy-done | bytes 131096
  2.4 0.0 copy-start.2
  2.4 0.9 %copy-done.2 = f32[32,8,128]{2,1,0:T(8,128)S(1)} copy-done((f32[32,8,128]{2,1,0:T(8,128)S(1)}, f32[32,8,128]{2,1,0:T(8,128)}, u32[]{:S(2)}) %copy-start.2) | copy-done | bytes 131096
  3.4 0.0 copy-start.3
  3.4 0.9 %copy-done.3 = f32[32,8,128]{2,1,0:T(8,128)S(1)} copy-done((f32[32,8,128]{2,1,0:T(8,128)S(1)}, f32[32,8,128]{2,1,0:T(8,128)}, u32[]{:S(2)}) %copy-start.3) | copy-done | bytes 131096
  4.3 0.0 copy-start.4
  4.3 0.7 %copy-done.4 = s32[8,128]{1,0:T(8,128)S(1)} copy-done((s32[8,128]{1,0:T(8,128)S(1)}, s32[8,128]{1,0:T(8,128)}, u32[]{:S(2)}) %copy-start.4) | copy-done | bytes 4120
  4.9 0.0 copy-start.5
  4.9 0.7 %copy-done.5 = f32[8,128]{1,0:T(8,128)S(1)} copy-done((f32[8,128]{1,0:T(8,128)S(1)}, f32[8,128]{1,0:T(8,128)}, u32[]{:S(2)}) %copy-start.5) | copy-done | bytes 4120
  5.6 0.0 copy-start.6
  5.6 0.7 %copy-done.6 = f32[8,128]{1,0:T(8,128)S(1)} copy-done((f32[8,128]{1,0:T(8,128)S(1)}, f32[8,128]{1,0:T(8,128)}, u32[]{:S(2)}) %copy-start.6) | copy-done | bytes 4120
  6.3 0.0 copy-start.7
  6.3 0.7 %copy-done.7 = f32[8,128]{1,0:T(8,128)S(1)} copy-done((f32[8,128]{1,0:T(8,128)S(1)}, f32[8,128]{1,0:T(8,128)}, u32[]{:S(2)}) %copy-start.7) | copy-done | bytes 4120
  7.0 39.3 %shard_map.135 = (f32[8,128]{1,0:T(8,128)S(1)}, f32[8,128]{1,0:T(8,128)S(1)}, f32[8,128]{1,0:T(8,128)S(1)}, f32[32,8,128]{2,1,0:T(8,128)S(1)}, f32[32,8,128]{2,1...) custom-call(s32[8,128]{1,0:T(8,128)S(1)} %copy-done.4, f32[8,128]{1,0:T(8,128)S(1)} %copy-done.5, ...), custom_call_target="tpu_custom_call" | custom-call | tf_op jit(solution)/shard_map/pallas_call | solution.py:285
  46.3 0.6 %copy.22 = f32[8,128]{1,0:T(8,128)} copy(f32[8,128]{1,0:T(8,128)S(1)} %get-tuple-element.14) | data formatting | bytes 8192
  46.9 0.6 %copy.23 = f32[8,128]{1,0:T(8,128)} copy(f32[8,128]{1,0:T(8,128)S(1)} %get-tuple-element.15) | data formatting | bytes 8192
  47.5 0.6 %copy.24 = f32[8,128]{1,0:T(8,128)} copy(f32[8,128]{1,0:T(8,128)S(1)} %get-tuple-element.16) | data formatting | bytes 8192
  48.1 0.7 %copy.25 = f32[32,8,128]{2,1,0:T(8,128)} copy(f32[32,8,128]{2,1,0:T(8,128)S(1)} %get-tuple-element.17) | data formatting | bytes 262144
  48.8 0.7 %copy.26 = f32[32,8,128]{2,1,0:T(8,128)} copy(f32[32,8,128]{2,1,0:T(8,128)S(1)} %get-tuple-element.18) | data formatting | bytes 262144
  49.4 0.7 %copy.27 = f32[32,8,128]{2,1,0:T(8,128)} copy(f32[32,8,128]{2,1,0:T(8,128)S(1)} %get-tuple-element.19) | data formatting | bytes 262144
  50.1 0.7 %copy.28 = f32[32,8,128]{2,1,0:T(8,128)} copy(f32[32,8,128]{2,1,0:T(8,128)S(1)} %get-tuple-element.20) | data formatting | bytes 262144
Async XLA Ops:
  0.6 0.9 %copy-start = (f32[32,8,128]{2,1,0:T(8,128)S(1)}, f32[32,8,128]{2,1,0:T(8,128)}, u32[]{:S(2)}) copy-start(f32[32,8,128]{2,1,0:T(8,128)} %x_hbm.1) | copy-start | bytes 393220
  1.5 0.9 %copy-start.1 = (f32[32,8,128]{2,1,0:T(8,128)S(1)}, f32[32,8,128]{2,1,0:T(8,128)}, u32[]{:S(2)}) copy-start(f32[32,8,128]{2,1,0:T(8,128)} %y_hbm.1) | copy-start | bytes 393220
  2.4 0.9 %copy-start.2 = (f32[32,8,128]{2,1,0:T(8,128)S(1)}, f32[32,8,128]{2,1,0:T(8,128)}, u32[]{:S(2)}) copy-start(f32[32,8,128]{2,1,0:T(8,128)} %t_hbm.1) | copy-start | bytes 393220
  3.4 0.9 %copy-start.3 = (f32[32,8,128]{2,1,0:T(8,128)S(1)}, f32[32,8,128]{2,1,0:T(8,128)}, u32[]{:S(2)}) copy-start(f32[32,8,128]{2,1,0:T(8,128)} %s_hbm.1) | copy-start | bytes 393220
  4.3 0.7 %copy-start.4 = (s32[8,128]{1,0:T(8,128)S(1)}, s32[8,128]{1,0:T(8,128)}, u32[]{:S(2)}) copy-start(s32[8,128]{1,0:T(8,128)} %bottom_hbm.1) | copy-start | bytes 12292
  4.9 0.7 %copy-start.5 = (f32[8,128]{1,0:T(8,128)S(1)}, f32[8,128]{1,0:T(8,128)}, u32[]{:S(2)}) copy-start(f32[8,128]{1,0:T(8,128)} %level_hbm.1) | copy-start | bytes 12292
  5.6 0.7 %copy-start.6 = (f32[8,128]{1,0:T(8,128)S(1)}, f32[8,128]{1,0:T(8,128)}, u32[]{:S(2)}) copy-start(f32[8,128]{1,0:T(8,128)} %flow_x_hbm.1) | copy-start | bytes 12292
  6.3 0.7 %copy-start.7 = (f32[8,128]{1,0:T(8,128)S(1)}, f32[8,128]{1,0:T(8,128)}, u32[]{:S(2)}) copy-start(f32[8,128]{1,0:T(8,128)} %flow_y_hbm.1) | copy-start | bytes 12292

commit v2 on v1

--- a/solution.py
+++ b/solution.py
@@ -1,5 +1,3 @@
-import functools
-
 import jax
 import jax.numpy as jnp
 from jax import lax
@@ -25,7 +23,7 @@
 
 def kernel(
     bottom_hbm, level_hbm, flow_x_hbm, flow_y_hbm, x_hbm, y_hbm, t_hbm, s_hbm,
-    level_out, east_out, north_out, x_out, y_out, t_out, s_out,
+    flat_out, x_out, y_out, t_out, s_out,
     bottom, own, big, edge, side_recv, stack_recv,
     row_first, row_last, row_north, row_south,
     col_to_east, col_to_west, col_from_west, col_from_east,
@@ -77,27 +75,6 @@
         packed = jnp.where(lane // 32 == i, roll(own[i], EDGE + 32 * i), packed)
     edge[...] = packed
 
-    for copy in large:
-        copy.wait()
-    for i in range(4):
-        row_first[pl.ds(i * LEVELS, LEVELS), :] = big[i, :, 0, :]
-        row_last[pl.ds(i * LEVELS, LEVELS), :] = big[i, :, ROWS - 1, :]
-
-    def pack(k, carry):
-        first, second = carry
-        first = jnp.where(lane // 2 == k, pltpu.roll(big[0, k], 2 * k + 1, 1), first)
-        first = jnp.where(lane // 2 == k + 32, pltpu.roll(big[1, k], 2 * k + 65, 1), first)
-        second = jnp.where(lane // 2 == k, pltpu.roll(big[2, k], 2 * k + 1, 1), second)
-        second = jnp.where(
-            lane // 2 == k + 32, pltpu.roll(big[3, k], (2 * k + 65) % COLS, 1), second
-        )
-        return first, second
-
-    zero = jnp.zeros((ROWS, COLS), f32)
-    first, second = lax.fori_loop(0, LEVELS, pack, (zero, zero), unroll=LEVELS)
-    col_to_east[...] = jnp.where(even, first, roll(second, 1))
-    col_to_west[...] = jnp.where(even, roll(first, -1), second)
-
     pl.semaphore_wait(barrier, len(OFFSETS))
 
     copies = []
@@ -120,6 +97,27 @@
     for a, o in STACKS:
         slot = STACKS.index((-a, -o))
         send(own, stack_recv.at[slot], len(SIDES) + slot, (a, o))
+    for copy in large:
+        copy.wait()
+    for i in range(4):
+        row_first[pl.ds(i * LEVELS, LEVELS), :] = big[i, :, 0, :]
+        row_last[pl.ds(i * LEVELS, LEVELS), :] = big[i, :, ROWS - 1, :]
+
+    def pack(k, carry):
+        first, second = carry
+        first = jnp.where(lane // 2 == k, pltpu.roll(big[0, k], 2 * k + 1, 1), first)
+        first = jnp.where(lane // 2 == k + 32, pltpu.roll(big[1, k], 2 * k + 65, 1), first)
+        second = jnp.where(lane // 2 == k, pltpu.roll(big[2, k], 2 * k + 1, 1), second)
+        second = jnp.where(
+            lane // 2 == k + 32, pltpu.roll(big[3, k], (2 * k + 65) % COLS, 1), second
+        )
+        return first, second
+
+    zero = jnp.zeros((ROWS, COLS), f32)
+    first, second = lax.fori_loop(0, LEVELS, pack, (zero, zero), unroll=LEVELS)
+    col_to_east[...] = jnp.where(even, first, roll(second, 1))
+    col_to_west[...] = jnp.where(even, roll(first, -1), second)
+
     halo_count = len(OFFSETS)
     send(col_to_east, col_from_west, halo_count, (0, 1))
     send(col_to_west, col_from_east, halo_count + 1, (0, -1))
@@ -214,9 +212,9 @@
                 cells[ROWS : 4 * ROWS] for cells in (wet, gain, level, flow_x, flow_y)
             )
     level, flow_x, flow_y = (cells[ROWS : 2 * ROWS, :COLS] for cells in (level, flow_x, flow_y))
-    level_out[...] = level
-    east_out[...] = flow_x
-    north_out[...] = flow_y
+    flat_out[0] = level
+    flat_out[1] = flow_x
+    flat_out[2] = flow_y
 
     for copy in copies[halo_count:]:
         copy.wait_recv()
@@ -278,15 +276,30 @@
         copy.wait_send()
 
 
+def store(flat, x, y, t, s, *rest):
+    outs, sem = rest[:-1], rest[-1]
+    sources = [flat.at[i] for i in range(3)] + [x, y, t, s]
+    copies = [
+        pltpu.make_async_copy(source, out, sem.at[i])
+        for i, (source, out) in enumerate(zip(sources, outs))
+    ]
+    for copy in copies:
+        copy.start()
+    for copy in copies:
+        copy.wait()
+
+
 def body(*args):
     flat = jax.ShapeDtypeStruct((ROWS, COLS), f32)
     deep = jax.ShapeDtypeStruct((LEVELS, ROWS, COLS), f32)
     messages = len(OFFSETS) + 4
-    return pl.pallas_call(
+    args = [pltpu.with_memory_space_constraint(arg, pltpu.HBM) for arg in args]
+    held = pl.pallas_call(
         kernel,
-        out_shape=(flat,) * 3 + (deep,) * 4,
-        in_specs=[pl.BlockSpec(memory_space=pl.ANY)] * 8,
-        out_specs=(pl.BlockSpec(memory_space=pltpu.VMEM),) * 7,
+        out_shape=(pltpu.VMEM((3, ROWS, COLS), f32),)
+        + (pltpu.VMEM((LEVELS, ROWS, COLS), f32),) * 4,
+        in_specs=[pl.BlockSpec(memory_space=pltpu.HBM)] * 8,
+        out_specs=(pl.BlockSpec(memory_space=pltpu.VMEM),) * 5,
         scratch_shapes=[
             pltpu.VMEM((ROWS, COLS), jnp.int32),
             pltpu.VMEM((4, ROWS, COLS), f32),
@@ -309,7 +322,16 @@
         compiler_params=pltpu.CompilerParams(
             collective_id=0, has_side_effects=True, vmem_limit_bytes=16 * 1024 * 1024
         ),
+        name="step",
     )(*args)
+    return pl.pallas_call(
+        store,
+        out_shape=(flat,) * 3 + (deep,) * 4,
+        in_specs=[pl.BlockSpec(memory_space=pltpu.VMEM)] * 5,
+        out_specs=(pl.BlockSpec(memory_space=pltpu.HBM),) * 7,
+        scratch_shapes=[pltpu.SemaphoreType.DMA((7,))],
+        name="store",
+    )(*held)
 
 
 def solution(mesh):

time: 51.1 us -> 45.3 us (0.89)
  local copies, waits for them, and re-layouts: 10.8 us -> 3.17 us
  Pallas kernels: 39.3 us -> 41.3 us
    unnamed x23 -> x10, local copies, waits for them, and re-layouts: 10.8 us -> 3.17 us
    pallas_call x1 -> x2, Pallas kernels: 39.3 us -> 41.3 us  [the longest x1 39.3 us: body(): pl.pallas_call(kernel, out_shape=(pltpu.VMEM((3, ROWS, COLS), f32),) + (p...]
where the time goes in v2:
time: 45.3 us; the launch traced here: 45.1 us
  Pallas kernels  41.3 us (91%)
  local copies, waits for them, and re-layouts  3.17 us (7%)
  between operations  0.66 us (1%)
    pallas_call x1, Pallas kernels, body(): pl.pallas_call(kernel, out_shape=(pltpu.VMEM((3, ROWS, COLS), f32),) + (p...  39.3 us
    unnamed x10, local copies, waits for them, and re-layouts  3.17 us
    pallas_call x1, Pallas kernels, body(): pl.pallas_call(store, out_shape=(flat,) * 3 + (deep,) * 4, in_specs=[pl.B...  1.96 us

profile of v2, /device:TPU:1, one launch (start us, length us, event | category | flops | bytes accessed | tf_op | source)
XLA Modules:
  0.0 45.1 jit_solution(5994610012037305611)
XLA Ops:
  0.6 39.3 %step.1 = (f32[3,8,128]{2,1,0:T(8,128)S(1)}, f32[32,8,128]{2,1,0:T(8,128)S(1)}, f32[32,8,128]{2,1,0:T(8,128)S(1)}, f32[32,8,128]{2,1,0:T(8,128)S(1)}, f32[32,8,128]{2,1,0:T(8,128)S(1)}) custom-call(s32[8,128]{1,0:T(8,128)} %bottom_hbm.1, f32[8,128]{1,0:T(8,128)} %level_hbm.1, f32[8,128]{1,0:T(8,128)} %flow_x_hbm.1, f32[8,128]{1,0:T(8,128)} %flow_y_hbm.1, ...), custom_call_target="tpu_custom_call" | custom-call | tf_op jit(solution)/shard_map/step/pallas_call | solution.py:297
  40.0 0.0 copy-start
  40.0 0.6 %copy-done = f32[32,8,128]{2,1,0:T(8,128)} copy-done((f32[32,8,128]{2,1,0:T(8,128)}, f32[32,8,128]{2,1,0:T(8,128)S(1)}, u32[]{:S(2)}) %copy-start) | copy-done | bytes 131096
  40.6 0.0 copy-start.1
  40.6 0.6 %copy-done.1 = f32[32,8,128]{2,1,0:T(8,128)} copy-done((f32[32,8,128]{2,1,0:T(8,128)}, f32[32,8,128]{2,1,0:T(8,128)S(1)}, u32[]{:S(2)}) %copy-start.1) | copy-done | bytes 131096
  41.3 0.0 copy-start.2
  41.3 0.6 %copy-done.2 = f32[32,8,128]{2,1,0:T(8,128)} copy-done((f32[32,8,128]{2,1,0:T(8,128)}, f32[32,8,128]{2,1,0:T(8,128)S(1)}, u32[]{:S(2)}) %copy-start.2) | copy-done | bytes 131096
  41.9 0.0 copy-start.3
  41.9 0.6 %copy-done.3 = f32[32,8,128]{2,1,0:T(8,128)} copy-done((f32[32,8,128]{2,1,0:T(8,128)}, f32[32,8,128]{2,1,0:T(8,128)S(1)}, u32[]{:S(2)}) %copy-start.3) | copy-done | bytes 131096
  42.6 0.0 copy-start.4
  42.6 0.6 %copy-done.4 = f32[3,8,128]{2,1,0:T(8,128)} copy-done((f32[3,8,128]{2,1,0:T(8,128)}, f32[3,8,128]{2,1,0:T(8,128)S(1)}, u32[]{:S(2)}) %copy-start.4) | copy-done | bytes 12312
  43.2 2.0 %store.1 = (f32[8,128]{1,0:T(8,128)}, f32[8,128]{1,0:T(8,128)}, f32[8,128]{1,0:T(8,128)}, f32[32,8,128]{2,1,0:T(8,128)}, f32[32,8,128]{2,1,0:T(8,128)}, /*index=5*/f32[32,8,128]{2,1,0:T(8,128)}, f32[32,8,128]{2,1,0:T(8,128)}) custom-call(f32[3,8,128]{2,1,0:T(8,128)} %copy-done.4, f32[32,8,128]{2,1,0:T(8,128)} %copy-done, f32[32,8,128]{2,1,0:T(8,128)} %copy-done.1, ...), custom_call_target="tpu_custom_call" | custom-call | tf_op jit(solution)/shard_map/store/pallas_call | solution.py:327
Async XLA Ops:
  40.0 0.6 %copy-start = (f32[32,8,128]{2,1,0:T(8,128)}, f32[32,8,128]{2,1,0:T(8,128)S(1)}, u32[]{:S(2)}) copy-start(f32[32,8,128]{2,1,0:T(8,128)S(1)} %get-tuple-element.13.x) | copy-start | bytes 393220
  40.6 0.7 %copy-start.1 = (f32[32,8,128]{2,1,0:T(8,128)}, f32[32,8,128]{2,1,0:T(8,128)S(1)}, u32[]{:S(2)}) copy-start(f32[32,8,128]{2,1,0:T(8,128)S(1)} %get-tuple-element.14.y) | copy-start | bytes 393220
  41.3 0.6 %copy-start.2 = (f32[32,8,128]{2,1,0:T(8,128)}, f32[32,8,128]{2,1,0:T(8,128)S(1)}, u32[]{:S(2)}) copy-start(f32[32,8,128]{2,1,0:T(8,128)S(1)} %get-tuple-element.15.t) | copy-start | bytes 393220
  41.9 0.6 %copy-start.3 = (f32[32,8,128]{2,1,0:T(8,128)}, f32[32,8,128]{2,1,0:T(8,128)S(1)}, u32[]{:S(2)}) copy-start(f32[32,8,128]{2,1,0:T(8,128)S(1)} %get-tuple-element.16.s) | copy-start | bytes 393220
  42.6 0.6 %copy-start.4 = (f32[3,8,128]{2,1,0:T(8,128)}, f32[3,8,128]{2,1,0:T(8,128)S(1)}, u32[]{:S(2)}) copy-start(f32[3,8,128]{2,1,0:T(8,128)S(1)} %get-tuple-element.12.flat) | copy-start | bytes 36868

commit v3 on v2

--- a/solution.py
+++ b/solution.py
@@ -13,11 +13,13 @@
 WAVE = 0.45
 CORIOLIS = 0.12
 DIAPYCNAL = 0.2
-UNROLL = 4
-
-SIDES = [(a, o) for o in (-1, 1) for a in (-2, -1, 0, 1, 2)]
-STACKS = [(a, 0) for a in (-2, -1, 1, 2)]
-OFFSETS = SIDES + STACKS
+
+LATS = (-2, -1, 0, 1, 2)
+OFFSETS = (
+    (0, 1), (1, 0), (1, 1), (2, 0), (2, 1),
+    (-1, 0), (-1, 1), (-2, 0), (-2, 1),
+    (0, -1), (1, -1), (2, -1), (-1, -1), (-2, -1),
+)
 f32 = jnp.float32
 
 
@@ -25,24 +27,50 @@
     bottom_hbm, level_hbm, flow_x_hbm, flow_y_hbm, x_hbm, y_hbm, t_hbm, s_hbm,
     flat_out, x_out, y_out, t_out, s_out,
     bottom, own, big, edge, side_recv, stack_recv,
-    row_first, row_last, row_north, row_south,
-    col_to_east, col_to_west, col_from_west, col_from_east,
+    rows_send, rows_recv, cols_send, cols_recv,
     local_sem, send_sem, recv_sem,
 ):
     lat, lon = lax.axis_index("lat"), lax.axis_index("lon")
     lats, lons = lax.axis_size("lat"), lax.axis_size("lon")
 
-    def place(offset):
-        return {
-            "lat": lax.rem(lat + offset[0] + lats, lats),
-            "lon": lax.rem(lon + offset[1] + lons, lons),
-        }
+    def flag(condition):
+        return jnp.where(condition, 1, 0)
+
+    spot, core = lax.rem(lat, 8), lax.rem(lon, 2)
+    within = lax.rem(lon, 8)
+    seam = flag(within == 0) + flag(within == 7)
+    western = lax.rem(lax.div(lon, 8) + 3 + core, 4)
+    up, across = 1 - 2 * flag(spot >= 4), 1 - 2 * core
+
+    def roles(a_sign, o_sign):
+        a, o = a_sign * up, o_sign * across
+        if o_sign == 0:
+            lead = flag(spot < lax.rem(lat + a + lats, 8))
+            return a, o, lead, 1 - lead
+        if o_sign == 1:
+            return a, o, core, 1 - core
+        far = core * flag(spot + a < 0) + (1 - core) * flag(spot + a >= 8)
+        west = flag(western == 0) + flag(western == 1) * (1 - far)
+        east = flag(western == 3)
+        lead = core * west + (1 - core) * east
+        trail = core * east + (1 - core) * west
+        return a, o, seam * lead + (1 - seam) * core, seam * trail + (1 - seam) * (1 - core)
+
+    neighbours = [(sign, *roles(*sign)) for sign in OFFSETS]
+
+    def place(a, o):
+        return {"lat": lax.rem(lat + a + lats, lats), "lon": lax.rem(lon + o + lons, lons)}
 
     barrier = pltpu.get_barrier_semaphore()
-    for offset in OFFSETS:
-        pl.semaphore_signal(
-            barrier, inc=1, device_id=place(offset), device_id_type=pl.DeviceIdType.MESH
-        )
+    for _, a, o, _, trail in neighbours[::-1]:
+
+        @pl.when(trail == 0)
+        def _(a=a, o=o):
+            pl.semaphore_signal(
+                barrier, inc=1, device_id=place(a, o), device_id_type=pl.DeviceIdType.MESH
+            )
+
+    awaited = sum(1 - lead for _, _, _, lead, _ in neighbours)
 
     small = [
         pltpu.make_async_copy(bottom_hbm, bottom, local_sem.at[0]),
@@ -75,33 +103,47 @@
         packed = jnp.where(lane // 32 == i, roll(own[i], EDGE + 32 * i), packed)
     edge[...] = packed
 
-    pl.semaphore_wait(barrier, len(OFFSETS))
-
-    copies = []
-
-    def send(src, dst, index, offset):
-        copy = pltpu.make_async_remote_copy(
+    def message(src, dst, index, a, o):
+        return pltpu.make_async_remote_copy(
             src_ref=src,
             dst_ref=dst,
             send_sem=send_sem.at[index],
             recv_sem=recv_sem.at[index],
-            device_id=place(offset),
+            device_id=place(a, o),
             device_id_type=pl.DeviceIdType.MESH,
         )
-        copy.start()
-        copies.append(copy)
-
-    for a, o in SIDES:
-        slot = SIDES.index((-a, -o))
-        send(edge, side_recv.at[slot], slot, (a, o))
-    for a, o in STACKS:
-        slot = STACKS.index((-a, -o))
-        send(own, stack_recv.at[slot], len(SIDES) + slot, (a, o))
+
+    def halo(sign, a, o):
+        if sign[1] == 0:
+            return message(own, stack_recv.at[2 - a], 12 - a, a, o)
+        slot = 2 - a + 5 * lax.div(1 - o, 2)
+        return message(edge, side_recv.at[slot], slot, a, o)
+
+    def deep_edge(sign, a, o):
+        if sign[1] == 0:
+            there, slot = lax.div(a + 1, 2), lax.div(1 - a, 2)
+            return message(rows_send.at[there], rows_recv.at[slot], 15 + slot, a, o)
+        there, slot = lax.div(o + 1, 2), lax.div(1 - o, 2)
+        return message(cols_send.at[there], cols_recv.at[slot], 17 + slot, a, o)
+
+    def adjacent(sign):
+        return abs(sign[0]) + abs(sign[1]) == 1
+
+    @pl.when(awaited > 0)
+    def _():
+        pl.semaphore_wait(barrier, awaited)
+
+    for sign, a, o, lead, _ in neighbours[::-1]:
+
+        @pl.when(lead == 0)
+        def _(sign=sign, a=a, o=o):
+            halo(sign, a, o).start()
+
     for copy in large:
         copy.wait()
     for i in range(4):
-        row_first[pl.ds(i * LEVELS, LEVELS), :] = big[i, :, 0, :]
-        row_last[pl.ds(i * LEVELS, LEVELS), :] = big[i, :, ROWS - 1, :]
+        rows_send[0, pl.ds(i * LEVELS, LEVELS), :] = big[i, :, 0, :]
+        rows_send[1, pl.ds(i * LEVELS, LEVELS), :] = big[i, :, ROWS - 1, :]
 
     def pack(k, carry):
         first, second = carry
@@ -115,14 +157,15 @@
 
     zero = jnp.zeros((ROWS, COLS), f32)
     first, second = lax.fori_loop(0, LEVELS, pack, (zero, zero), unroll=LEVELS)
-    col_to_east[...] = jnp.where(even, first, roll(second, 1))
-    col_to_west[...] = jnp.where(even, roll(first, -1), second)
-
-    halo_count = len(OFFSETS)
-    send(col_to_east, col_from_west, halo_count, (0, 1))
-    send(col_to_west, col_from_east, halo_count + 1, (0, -1))
-    send(row_last, row_south, halo_count + 2, (1, 0))
-    send(row_first, row_north, halo_count + 3, (-1, 0))
+    cols_send[1] = jnp.where(even, first, roll(second, 1))
+    cols_send[0] = jnp.where(even, roll(first, -1), second)
+
+    for sign, a, o, lead, _ in neighbours:
+        if adjacent(sign):
+
+            @pl.when(lead == 0)
+            def _(sign=sign, a=a, o=o):
+                deep_edge(sign, a, o).start()
 
     centre = own[0]
     coef = 0.08 + (0.12 / LEVELS) * centre
@@ -164,22 +207,32 @@
             out[k] = cells + coef * lateral(cells) + DIAPYCNAL * vertical
         return press, sum_x + jnp.where(wet, x, 0.0), sum_y + jnp.where(wet, y, 0.0)
 
-    _, sum_x, sum_y = lax.fori_loop(0, LEVELS, inner, (zero, zero, zero), unroll=UNROLL)
+    _, sum_x, sum_y = lax.fori_loop(0, LEVELS, inner, (zero, zero, zero), unroll=LEVELS)
     count = jnp.maximum(centre, 1.0)
     mean_x, mean_y = sum_x / count, sum_y / count
 
-    for copy in copies[:halo_count]:
-        copy.wait_recv()
+    for sign, a, o, lead, _ in neighbours:
+
+        @pl.when(lead == 1)
+        def _(sign=sign, a=a, o=o):
+            halo(sign, -a, -o).wait_recv()
+            halo(sign, a, o).start()
+            if adjacent(sign):
+                deep_edge(sign, a, o).start()
+
+    for sign, a, o, lead, _ in neighbours:
+
+        @pl.when(lead == 0)
+        def _(sign=sign, a=a, o=o):
+            halo(sign, -a, -o).wait_recv()
 
     fields = [[], [], [], []]
     for a in (-2, -1, 0, 1, 2):
         inside = (lat + a >= 0) & (lat + a < lats)
         keep = jnp.where(inside, 1.0, 0.0).astype(f32)
-        merged = jnp.where(
-            lane % 32 < EDGE, side_recv[SIDES.index((a, -1))], side_recv[SIDES.index((a, 1))]
-        )
+        merged = jnp.where(lane % 32 < EDGE, side_recv[a + 2], side_recv[a + 7])
         for i in range(4):
-            middle = own[i] if a == 0 else stack_recv[STACKS.index((a, 0)), i]
+            middle = own[i] if a == 0 else stack_recv[a + 2, i]
             beside = roll(merged, -(EDGE + 32 * i))
             if i == 0 and a != 0:
                 middle, beside = middle * keep, beside * keep
@@ -216,8 +269,9 @@
     flat_out[1] = flow_x
     flat_out[2] = flow_y
 
-    for copy in copies[halo_count:]:
-        copy.wait_recv()
+    for sign, a, o, _, _ in neighbours:
+        if adjacent(sign):
+            deep_edge(sign, -a, -o).wait_recv()
 
     beside = halo_bottom[2][1]
     bottom_ew = jnp.where(
@@ -228,7 +282,7 @@
         slide(halo_bottom[3][0], -1),
         jnp.where(row == 0, slide(halo_bottom[1][0], 1), 0.0),
     )
-    from_east, from_west = col_from_east[...], col_from_west[...]
+    from_west, from_east = cols_recv[0], cols_recv[1]
     first = jnp.where(even, from_east, roll(from_west, 1))
     second = jnp.where(even, roll(from_east, -1), from_west)
     sign_ew = jnp.where(lane == COLS - 1, 1.0, -1.0)
@@ -250,8 +304,8 @@
         stacks = [
             jnp.where(
                 upper,
-                jnp.broadcast_to(row_south[pl.ds(i * LEVELS + k, 1), :], (ROWS, COLS)),
-                jnp.broadcast_to(row_north[pl.ds(i * LEVELS + k, 1), :], (ROWS, COLS)),
+                jnp.broadcast_to(rows_recv[0, pl.ds(i * LEVELS + k, 1), :], (ROWS, COLS)),
+                jnp.broadcast_to(rows_recv[1, pl.ds(i * LEVELS + k, 1), :], (ROWS, COLS)),
             )
             for i in range(4)
         ]
@@ -270,10 +324,12 @@
         s_out[k] = jnp.where(wet, s_out[k] + coef * lateral(3), 0.0)
         return press_ew, press_ns
 
-    lax.fori_loop(0, LEVELS, outer, (zero, zero), unroll=UNROLL)
-
-    for copy in copies:
-        copy.wait_send()
+    lax.fori_loop(0, LEVELS, outer, (zero, zero), unroll=LEVELS)
+
+    for sign, a, o, _, _ in neighbours:
+        halo(sign, a, o).wait_send()
+        if adjacent(sign):
+            deep_edge(sign, a, o).wait_send()
 
 
 def store(flat, x, y, t, s, *rest):
@@ -292,7 +348,7 @@
 def body(*args):
     flat = jax.ShapeDtypeStruct((ROWS, COLS), f32)
     deep = jax.ShapeDtypeStruct((LEVELS, ROWS, COLS), f32)
-    messages = len(OFFSETS) + 4
+    messages = 19
     args = [pltpu.with_memory_space_constraint(arg, pltpu.HBM) for arg in args]
     held = pl.pallas_call(
         kernel,
@@ -305,16 +361,12 @@
             pltpu.VMEM((4, ROWS, COLS), f32),
             pltpu.VMEM((4, LEVELS, ROWS, COLS), f32),
             pltpu.VMEM((ROWS, COLS), f32),
-            pltpu.VMEM((len(SIDES), ROWS, COLS), f32),
-            pltpu.VMEM((len(STACKS), 4, ROWS, COLS), f32),
-            pltpu.VMEM((4 * LEVELS, COLS), f32),
-            pltpu.VMEM((4 * LEVELS, COLS), f32),
-            pltpu.VMEM((4 * LEVELS, COLS), f32),
-            pltpu.VMEM((4 * LEVELS, COLS), f32),
-            pltpu.VMEM((ROWS, COLS), f32),
-            pltpu.VMEM((ROWS, COLS), f32),
-            pltpu.VMEM((ROWS, COLS), f32),
-            pltpu.VMEM((ROWS, COLS), f32),
+            pltpu.VMEM((10, ROWS, COLS), f32),
+            pltpu.VMEM((5, 4, ROWS, COLS), f32),
+            pltpu.VMEM((2, 4 * LEVELS, COLS), f32),
+            pltpu.VMEM((2, 4 * LEVELS, COLS), f32),
+            pltpu.VMEM((2, ROWS, COLS), f32),
+            pltpu.VMEM((2, ROWS, COLS), f32),
             pltpu.SemaphoreType.DMA((8,)),
             pltpu.SemaphoreType.DMA((messages,)),
             pltpu.SemaphoreType.DMA((messages,)),
@@ -330,8 +382,9 @@
         in_specs=[pl.BlockSpec(memory_space=pltpu.VMEM)] * 5,
         out_specs=(pl.BlockSpec(memory_space=pltpu.HBM),) * 7,
         scratch_shapes=[pltpu.SemaphoreType.DMA((7,))],
+        compiler_params=pltpu.CompilerParams(vmem_limit_bytes=1024 * 1024),
         name="store",
-    )(*held)
+    )(*(pltpu.with_memory_space_constraint(cells, pltpu.VMEM) for cells in held))
 
 
 def solution(mesh):

time: 45.3 us -> 33.7 us (0.74)
  the two profiles are of different devices: /device:TPU:1 before, /device:TPU:25 now
where the time goes in v3:
time: 33.7 us; the launch traced here: 33.5 us
  Pallas kernels  32.9 us (98%)
  between operations  0.64 us (2%)
    pallas_call x1, Pallas kernels, body(): pl.pallas_call(kernel, out_shape=(pltpu.VMEM((3, ROWS, COLS), f32),) + (p...  32 us
    pallas_call x1, Pallas kernels, body(): pl.pallas_call(store, out_shape=(flat,) * 3 + (deep,) * 4, in_specs=[pl.B...  0.86 us

profile of v3, /device:TPU:25, one launch (start us, length us, event | category | flops | bytes accessed | tf_op | source)
XLA Modules:
  0.0 33.5 jit_solution(7568121872729261546)
XLA Ops:
  0.6 32.0 %step.1 = (f32[3,8,128]{2,1,0:T(8,128)S(1)}, f32[32,8,128]{2,1,0:T(8,128)S(1)}, f32[32,8,128]{2,1,0:T(8,128)S(1)}, f32[32,8,128]{2,1,0:T(8,128)S(1)}, f32[32,8,128]{2,1,0:T(8,128)S(1)}) custom-call(s32[8,128]{1,0:T(8,128)} %bottom_hbm.1, f32[8,128]{1,0:T(8,128)} %level_hbm.1, f32[8,128]{1,0:T(8,128)} %flow_x_hbm.1, f32[8,128]{1,0:T(8,128)} %flow_y_hbm.1, ...), custom_call_target="tpu_custom_call" | custom-call | tf_op jit(solution)/shard_map/step/pallas_call | solution.py:353
  32.7 0.9 %store.1 = (f32[8,128]{1,0:T(8,128)}, f32[8,128]{1,0:T(8,128)}, f32[8,128]{1,0:T(8,128)}, f32[32,8,128]{2,1,0:T(8,128)}, f32[32,8,128]{2,1,0:T(8,128)}, /*index=5*/f32[32,8,128]{2,1,0:T(8,128)}, f32[32,8,128]{2,1,0:T(8,128)}) custom-call(f32[3,8,128]{2,1,0:T(8,128)S(1)} %get-tuple-element.12.flat, f32[32,8,128]{2,1,0:T(8,128)S(1)} %get-tuple-element.13.x, ...), custom_call_target="tpu_custom_call" | custom-call | tf_op jit(solution)/shard_map/store/pallas_call | solution.py:379

commit v4 on v3

--- a/solution.py
+++ b/solution.py
@@ -32,45 +32,6 @@
 ):
     lat, lon = lax.axis_index("lat"), lax.axis_index("lon")
     lats, lons = lax.axis_size("lat"), lax.axis_size("lon")
-
-    def flag(condition):
-        return jnp.where(condition, 1, 0)
-
-    spot, core = lax.rem(lat, 8), lax.rem(lon, 2)
-    within = lax.rem(lon, 8)
-    seam = flag(within == 0) + flag(within == 7)
-    western = lax.rem(lax.div(lon, 8) + 3 + core, 4)
-    up, across = 1 - 2 * flag(spot >= 4), 1 - 2 * core
-
-    def roles(a_sign, o_sign):
-        a, o = a_sign * up, o_sign * across
-        if o_sign == 0:
-            lead = flag(spot < lax.rem(lat + a + lats, 8))
-            return a, o, lead, 1 - lead
-        if o_sign == 1:
-            return a, o, core, 1 - core
-        far = core * flag(spot + a < 0) + (1 - core) * flag(spot + a >= 8)
-        west = flag(western == 0) + flag(western == 1) * (1 - far)
-        east = flag(western == 3)
-        lead = core * west + (1 - core) * east
-        trail = core * east + (1 - core) * west
-        return a, o, seam * lead + (1 - seam) * core, seam * trail + (1 - seam) * (1 - core)
-
-    neighbours = [(sign, *roles(*sign)) for sign in OFFSETS]
-
-    def place(a, o):
-        return {"lat": lax.rem(lat + a + lats, lats), "lon": lax.rem(lon + o + lons, lons)}
-
-    barrier = pltpu.get_barrier_semaphore()
-    for _, a, o, _, trail in neighbours[::-1]:
-
-        @pl.when(trail == 0)
-        def _(a=a, o=o):
-            pl.semaphore_signal(
-                barrier, inc=1, device_id=place(a, o), device_id_type=pl.DeviceIdType.MESH
-            )
-
-    awaited = sum(1 - lead for _, _, _, lead, _ in neighbours)
 
     small = [
         pltpu.make_async_copy(bottom_hbm, bottom, local_sem.at[0]),
@@ -85,6 +46,62 @@
     for copy in small + large:
         copy.start()
 
+    def flag(condition):
+        return jnp.where(condition, 1, 0)
+
+    spot, core = lax.rem(lat, 8), lax.rem(lon, 2)
+    within = lax.rem(lon, 8)
+    seam = flag(within == 0) + flag(within == 7)
+    western = lax.rem(lax.div(lon, 8) + 3 + core, 4)
+    up, across = 1 - 2 * flag(spot >= 4), 1 - 2 * core
+
+    def roles(a_sign, o_sign):
+        a, o = a_sign * up, o_sign * across
+        if o_sign == 0:
+            lead = flag(spot < lax.rem(lat + a + lats, 8))
+            return a, o, lead, 1 - lead
+        beyond = flag(spot + a < 0) + flag(spot + a >= 8)
+        near = jnp.where(
+            beyond == 0,
+            core,
+            jnp.where(lax.div(lon, 8) == 3, flag(o < 0), flag(spot < lax.rem(lat + a + lats, 8))),
+        )
+        if o_sign == 1:
+            return a, o, near, 1 - near
+        far = core * flag(spot + a < 0) + (1 - core) * flag(spot + a >= 8)
+        west = flag(western == 0) + flag(western == 1) * (1 - far)
+        east = flag(western == 3)
+        lead = core * west + (1 - core) * east
+        trail = core * east + (1 - core) * west
+        return a, o, jnp.where(seam == 1, lead, near), jnp.where(seam == 1, trail, 1 - near)
+
+    def is_first(a, o):
+        return flag(lax.rem(lat + a + lats, lats) + lax.rem(lon + o + lons, lons) == 0)
+
+    def settled(a_sign, o_sign):
+        a, o, lead, trail = roles(a_sign, o_sign)
+        if o_sign != -1:
+            lead = jnp.where(is_first(0, 0) == 1, 0, lead)
+            trail = jnp.where(is_first(0, 0) == 1, 1, trail)
+        first = is_first(a, o) * flag(o != 1)
+        return a, o, jnp.where(first == 1, 1, lead), jnp.where(first == 1, 0, trail)
+
+    neighbours = [(sign, *settled(*sign)) for sign in OFFSETS]
+
+    def place(a, o):
+        return {"lat": lax.rem(lat + a + lats, lats), "lon": lax.rem(lon + o + lons, lons)}
+
+    barrier = pltpu.get_barrier_semaphore()
+    for _, a, o, _, trail in neighbours[::-1]:
+
+        @pl.when(trail == 0)
+        def _(a=a, o=o):
+            pl.semaphore_signal(
+                barrier, inc=1, device_id=place(a, o), device_id_type=pl.DeviceIdType.MESH
+            )
+
+    awaited = sum(1 - lead for _, _, _, lead, _ in neighbours)
+
     lane = lax.broadcasted_iota(jnp.int32, (ROWS, COLS), 1)
     row = lax.broadcasted_iota(jnp.int32, (ROWS, COLS), 0)
     even = lane % 2 == 0
@@ -244,8 +261,8 @@
             [jnp.concatenate([m for m, _ in tiles], 0), jnp.concatenate([b for _, b in tiles], 0)], 1
         )
 
-    def ew(cells):
-        return pltpu.roll(cells, 2 * COLS - 1, 1) - pltpu.roll(cells, 1, 1)
+    def turn(cells, shift):
+        return pltpu.roll(cells, shift % (2 * COLS), 1)
 
     def ns(cells):
         return pltpu.roll(cells, cells.shape[0] - 1, 0) - pltpu.roll(cells, 1, 0)
@@ -254,15 +271,22 @@
     wet = jnp.where(column > 0.0, 1.0, 0.0)
     gain = (WAVE / LEVELS) * column
     level, flow_x, flow_y = wet * level, wet * flow_x, wet * flow_y
+    wet_e, wet_w = turn(wet, -1), turn(wet, 1)
     for cycle in range(SUBCYCLES):
-        level = level - wet * (ew(gain * flow_x) + ns(gain * flow_y))
+        flux_x = gain * flow_x
+        part = level - wet * ns(gain * flow_y)
+        level = part - wet * (turn(flux_x, -1) - turn(flux_x, 1))
+        slope_x = (turn(part, -1) - wet_e * (turn(flux_x, -2) - flux_x)) - (
+            turn(part, 1) - wet_w * (flux_x - turn(flux_x, 2))
+        )
         flow_x, flow_y = (
-            flow_x - gain * ew(level) + CORIOLIS * flow_y,
+            flow_x - gain * slope_x + CORIOLIS * flow_y,
             flow_y - gain * ns(level) - CORIOLIS * flow_x,
         )
         if cycle == 3:
-            wet, gain, level, flow_x, flow_y = (
-                cells[ROWS : 4 * ROWS] for cells in (wet, gain, level, flow_x, flow_y)
+            wet, wet_e, wet_w, gain, level, flow_x, flow_y = (
+                cells[ROWS : 4 * ROWS]
+                for cells in (wet, wet_e, wet_w, gain, level, flow_x, flow_y)
             )
     level, flow_x, flow_y = (cells[ROWS : 2 * ROWS, :COLS] for cells in (level, flow_x, flow_y))
     flat_out[0] = level

time: 33.7 us -> 33.2 us (0.985)
  Pallas kernels: 32.9 us -> 32.4 us
    pallas_call x1, Pallas kernels: 32 us -> 31.5 us  [body(): pl.pallas_call(kernel, out_shape=(pltpu.VMEM((3, ROWS, COLS), f32),) + (p...]
where the time goes in v4:
time: 33.2 us; the launch traced here: 33 us
  Pallas kernels  32.4 us (98%)
  between operations  0.64 us (2%)
    pallas_call x1, Pallas kernels, body(): pl.pallas_call(kernel, out_shape=(pltpu.VMEM((3, ROWS, COLS), f32),) + (p...  31.5 us
    pallas_call x1, Pallas kernels, body(): pl.pallas_call(store, out_shape=(flat,) * 3 + (deep,) * 4, in_specs=[pl.B...  0.86 us

profile of v4, /device:TPU:25, one launch (start us, length us, event | category | flops | bytes accessed | tf_op | source)
XLA Modules:
  0.0 33.0 jit_solution(7212086928455175901)
XLA Ops:
  0.6 31.5 %step.1 = (f32[3,8,128]{2,1,0:T(8,128)S(1)}, f32[32,8,128]{2,1,0:T(8,128)S(1)}, f32[32,8,128]{2,1,0:T(8,128)S(1)}, f32[32,8,128]{2,1,0:T(8,128)S(1)}, f32[32,8,128]{2,1,0:T(8,128)S(1)}) custom-call(s32[8,128]{1,0:T(8,128)} %bottom_hbm.1, f32[8,128]{1,0:T(8,128)} %level_hbm.1, f32[8,128]{1,0:T(8,128)} %flow_x_hbm.1, f32[8,128]{1,0:T(8,128)} %flow_y_hbm.1, ...), custom_call_target="tpu_custom_call" | custom-call | tf_op jit(solution)/shard_map/step/pallas_call | solution.py:377
  32.2 0.9 %store.1 = (f32[8,128]{1,0:T(8,128)}, f32[8,128]{1,0:T(8,128)}, f32[8,128]{1,0:T(8,128)}, f32[32,8,128]{2,1,0:T(8,128)}, f32[32,8,128]{2,1,0:T(8,128)}, /*index=5*/f32[32,8,128]{2,1,0:T(8,128)}, f32[32,8,128]{2,1,0:T(8,128)}) custom-call(f32[3,8,128]{2,1,0:T(8,128)S(1)} %get-tuple-element.12.flat, f32[32,8,128]{2,1,0:T(8,128)S(1)} %get-tuple-element.13.x, ...), custom_call_target="tpu_custom_call" | custom-call | tf_op jit(solution)/shard_map/store/pallas_call | solution.py:403

commit v5 on v4

--- a/solution.py
+++ b/solution.py
@@ -78,11 +78,20 @@
     def is_first(a, o):
         return flag(lax.rem(lat + a + lats, lats) + lax.rem(lon + o + lons, lons) == 0)
 
+    def awaits(a, o):
+        there = lax.rem(lon + o + lons, lons)
+        return flag(there == 24) * flag(lax.rem(lat + a + lats, 8) >= 6)
+
     def settled(a_sign, o_sign):
         a, o, lead, trail = roles(a_sign, o_sign)
         if o_sign != -1:
             lead = jnp.where(is_first(0, 0) == 1, 0, lead)
             trail = jnp.where(is_first(0, 0) == 1, 1, trail)
+        if o_sign != -1:
+            lead = jnp.where(awaits(0, 0) * flag(spot + a >= 8) == 1, 1, lead)
+            trail = jnp.where(awaits(0, 0) * flag(spot + a >= 8) == 1, 0, trail)
+        late = awaits(a, o) * flag(o != 1) * flag(spot + a < 0)
+        lead, trail = jnp.where(late == 1, 0, lead), jnp.where(late == 1, 1, trail)
         first = is_first(a, o) * flag(o != 1)
         return a, o, jnp.where(first == 1, 1, lead), jnp.where(first == 1, 0, trail)
 
@@ -242,6 +251,10 @@
         @pl.when(lead == 0)
         def _(sign=sign, a=a, o=o):
             halo(sign, -a, -o).wait_recv()
+
+    for sign, a, o, _, _ in neighbours:
+        if adjacent(sign):
+            deep_edge(sign, -a, -o).wait_recv()
 
     fields = [[], [], [], []]
     for a in (-2, -1, 0, 1, 2):
@@ -255,48 +268,6 @@
                 middle, beside = middle * keep, beside * keep
             fields[i].append((middle, beside))
     halo_bottom = fields[0]
-
-    def whole(tiles):
-        return jnp.concatenate(
-            [jnp.concatenate([m for m, _ in tiles], 0), jnp.concatenate([b for _, b in tiles], 0)], 1
-        )
-
-    def turn(cells, shift):
-        return pltpu.roll(cells, shift % (2 * COLS), 1)
-
-    def ns(cells):
-        return pltpu.roll(cells, cells.shape[0] - 1, 0) - pltpu.roll(cells, 1, 0)
-
-    column, level, flow_x, flow_y = (whole(tiles) for tiles in fields)
-    wet = jnp.where(column > 0.0, 1.0, 0.0)
-    gain = (WAVE / LEVELS) * column
-    level, flow_x, flow_y = wet * level, wet * flow_x, wet * flow_y
-    wet_e, wet_w = turn(wet, -1), turn(wet, 1)
-    for cycle in range(SUBCYCLES):
-        flux_x = gain * flow_x
-        part = level - wet * ns(gain * flow_y)
-        level = part - wet * (turn(flux_x, -1) - turn(flux_x, 1))
-        slope_x = (turn(part, -1) - wet_e * (turn(flux_x, -2) - flux_x)) - (
-            turn(part, 1) - wet_w * (flux_x - turn(flux_x, 2))
-        )
-        flow_x, flow_y = (
-            flow_x - gain * slope_x + CORIOLIS * flow_y,
-            flow_y - gain * ns(level) - CORIOLIS * flow_x,
-        )
-        if cycle == 3:
-            wet, wet_e, wet_w, gain, level, flow_x, flow_y = (
-                cells[ROWS : 4 * ROWS]
-                for cells in (wet, wet_e, wet_w, gain, level, flow_x, flow_y)
-            )
-    level, flow_x, flow_y = (cells[ROWS : 2 * ROWS, :COLS] for cells in (level, flow_x, flow_y))
-    flat_out[0] = level
-    flat_out[1] = flow_x
-    flat_out[2] = flow_y
-
-    for sign, a, o, _, _ in neighbours:
-        if adjacent(sign):
-            deep_edge(sign, -a, -o).wait_recv()
-
     beside = halo_bottom[2][1]
     bottom_ew = jnp.where(
         lane == COLS - 1, roll(beside, -1), jnp.where(lane == 0, roll(beside, 1), 0.0)
@@ -313,7 +284,6 @@
     sign_ns = jnp.where(row == ROWS - 1, 1.0, -1.0)
     t_ew, s_ew = 0.08 * sign_ew, -0.06 * sign_ew
     t_ns, s_ns = 0.08 * sign_ns, -0.06 * sign_ns
-    add_x, add_y = flow_x - mean_x, flow_y - mean_y
     upper = row < ROWS // 2
 
     def outer(k, carry):
@@ -342,13 +312,62 @@
 
         press_ew = press_ew + jnp.where(wet_ew, t_ew * sides[2] + s_ew * sides[3], 0.0)
         press_ns = press_ns + jnp.where(wet_ns, t_ns * stacks[2] + s_ns * stacks[3], 0.0)
-        x_out[k] = jnp.where(wet, x_out[k] + coef * lateral(0) + (press_ew + add_x), 0.0)
-        y_out[k] = jnp.where(wet, y_out[k] + coef * lateral(1) + (press_ns + add_y), 0.0)
+        x_out[k] = x_out[k] + coef * lateral(0) + press_ew
+        y_out[k] = y_out[k] + coef * lateral(1) + press_ns
         t_out[k] = jnp.where(wet, t_out[k] + coef * lateral(2), 0.0)
         s_out[k] = jnp.where(wet, s_out[k] + coef * lateral(3), 0.0)
         return press_ew, press_ns
 
-    lax.fori_loop(0, LEVELS, outer, (zero, zero), unroll=LEVELS)
+    edge_press = (zero, zero)
+
+
+    def whole(tiles):
+        return jnp.concatenate(
+            [jnp.concatenate([m for m, _ in tiles], 0), jnp.concatenate([b for _, b in tiles], 0)], 1
+        )
+
+    def turn(cells, shift):
+        return pltpu.roll(cells, shift % (2 * COLS), 1)
+
+    def ns(cells):
+        return pltpu.roll(cells, cells.shape[0] - 1, 0) - pltpu.roll(cells, 1, 0)
+
+    column, level, flow_x, flow_y = (whole(tiles) for tiles in fields)
+    wet = jnp.where(column > 0.0, 1.0, 0.0)
+    gain = (WAVE / LEVELS) * column
+    level, flow_x, flow_y = wet * level, wet * flow_x, wet * flow_y
+    wet_e, wet_w = turn(wet, -1), turn(wet, 1)
+    for cycle in range(SUBCYCLES):
+        flux_x = gain * flow_x
+        part = level - wet * ns(gain * flow_y)
+        level = part - wet * (turn(flux_x, -1) - turn(flux_x, 1))
+        slope_x = (turn(part, -1) - wet_e * (turn(flux_x, -2) - flux_x)) - (
+            turn(part, 1) - wet_w * (flux_x - turn(flux_x, 2))
+        )
+        flow_x, flow_y = (
+            flow_x - gain * slope_x + CORIOLIS * flow_y,
+            flow_y - gain * ns(level) - CORIOLIS * flow_x,
+        )
+        edge_press = lax.fori_loop(4 * cycle, 4 * cycle + 4, outer, edge_press, unroll=4)
+        if cycle == 3:
+            wet, wet_e, wet_w, gain, level, flow_x, flow_y = (
+                cells[ROWS : 4 * ROWS]
+                for cells in (wet, wet_e, wet_w, gain, level, flow_x, flow_y)
+            )
+    level, flow_x, flow_y = (cells[ROWS : 2 * ROWS, :COLS] for cells in (level, flow_x, flow_y))
+    flat_out[0] = level
+    flat_out[1] = flow_x
+    flat_out[2] = flow_y
+
+    add_x, add_y = flow_x - mean_x, flow_y - mean_y
+
+    def finish(k, carry):
+        wet = centre > lax.convert_element_type(k, f32)
+        x_out[k] = jnp.where(wet, x_out[k] + add_x, 0.0)
+        y_out[k] = jnp.where(wet, y_out[k] + add_y, 0.0)
+        return carry
+
+    lax.fori_loop(0, LEVELS, finish, 0, unroll=LEVELS)
 
     for sign, a, o, _, _ in neighbours:
         halo(sign, a, o).wait_send()

time: 33.2 us -> 33 us (level)
  no operation moved by 1% of the time
where the time goes in v5:
time: 33 us; the launch traced here: 32.8 us
  Pallas kernels  32.2 us (98%)
  between operations  0.64 us (2%)
    pallas_call x1, Pallas kernels, body(): pl.pallas_call(kernel, out_shape=(pltpu.VMEM((3, ROWS, COLS), f32),) + (p...  31.3 us
    pallas_call x1, Pallas kernels, body(): pl.pallas_call(store, out_shape=(flat,) * 3 + (deep,) * 4, in_specs=[pl.B...  0.86 us

profile of v5, /device:TPU:25, one launch (start us, length us, event | category | flops | bytes accessed | tf_op | source)
XLA Modules:
  0.0 32.8 jit_solution(4724246092902197969)
XLA Ops:
  0.6 31.3 %step.1 = (f32[3,8,128]{2,1,0:T(8,128)S(1)}, f32[32,8,128]{2,1,0:T(8,128)S(1)}, f32[32,8,128]{2,1,0:T(8,128)S(1)}, f32[32,8,128]{2,1,0:T(8,128)S(1)}, f32[32,8,128]{2,1,0:T(8,128)S(1)}) custom-call(s32[8,128]{1,0:T(8,128)} %bottom_hbm.1, f32[8,128]{1,0:T(8,128)} %level_hbm.1, f32[8,128]{1,0:T(8,128)} %flow_x_hbm.1, f32[8,128]{1,0:T(8,128)} %flow_y_hbm.1, ...), custom_call_target="tpu_custom_call" | custom-call | tf_op jit(solution)/shard_map/step/pallas_call | solution.py:396
  32.0 0.9 %store.1 = (f32[8,128]{1,0:T(8,128)}, f32[8,128]{1,0:T(8,128)}, f32[8,128]{1,0:T(8,128)}, f32[32,8,128]{2,1,0:T(8,128)}, f32[32,8,128]{2,1,0:T(8,128)}, /*index=5*/f32[32,8,128]{2,1,0:T(8,128)}, f32[32,8,128]{2,1,0:T(8,128)}) custom-call(f32[3,8,128]{2,1,0:T(8,128)S(1)} %get-tuple-element.12.flat, f32[32,8,128]{2,1,0:T(8,128)S(1)} %get-tuple-element.13.x, ...), custom_call_target="tpu_custom_call" | custom-call | tf_op jit(solution)/shard_map/store/pallas_call | solution.py:422

commit v6 on v5

--- a/solution.py
+++ b/solution.py
@@ -92,6 +92,12 @@
             trail = jnp.where(awaits(0, 0) * flag(spot + a >= 8) == 1, 0, trail)
         late = awaits(a, o) * flag(o != 1) * flag(spot + a < 0)
         lead, trail = jnp.where(late == 1, 0, lead), jnp.where(late == 1, 1, trail)
+        if o_sign == 0:
+            here = flag(lon == 8) * flag(spot + a >= 0) * flag(spot + a < 8)
+            ahead = here * flag(spot >= 6) * flag(spot + a < 6)
+            behind = here * flag(spot < 6) * flag(spot + a >= 6)
+            lead = jnp.where(ahead == 1, 1, jnp.where(behind == 1, 0, lead))
+            trail = jnp.where(ahead == 1, 0, jnp.where(behind == 1, 1, trail))
         first = is_first(a, o) * flag(o != 1)
         return a, o, jnp.where(first == 1, 1, lead), jnp.where(first == 1, 0, trail)
 
@@ -381,7 +387,7 @@
     copies = [
         pltpu.make_async_copy(source, out, sem.at[i])
         for i, (source, out) in enumerate(zip(sources, outs))
-    ]
+    ][::-1]
     for copy in copies:
         copy.start()
     for copy in copies:

time: 33 us -> 32.9 us (level)
  no operation moved by 1% of the time
where the time goes in v6:
time: 32.9 us; the launch traced here: 32.7 us
  Pallas kernels  32 us (97%)
  between operations  0.64 us (2%)
    pallas_call x1, Pallas kernels, body(): pl.pallas_call(kernel, out_shape=(pltpu.VMEM((3, ROWS, COLS), f32),) + (p...  31.2 us
    pallas_call x1, Pallas kernels, body(): pl.pallas_call(store, out_shape=(flat,) * 3 + (deep,) * 4, in_specs=[pl.B...  0.85 us

profile of v6, /device:TPU:25, one launch (start us, length us, event | category | flops | bytes accessed | tf_op | source)
XLA Modules:
  0.0 32.7 jit_solution(8485904449667848385)
XLA Ops:
  0.6 31.2 %step.1 = (f32[3,8,128]{2,1,0:T(8,128)S(1)}, f32[32,8,128]{2,1,0:T(8,128)S(1)}, f32[32,8,128]{2,1,0:T(8,128)S(1)}, f32[32,8,128]{2,1,0:T(8,128)S(1)}, f32[32,8,128]{2,1,0:T(8,128)S(1)}) custom-call(s32[8,128]{1,0:T(8,128)} %bottom_hbm.1, f32[8,128]{1,0:T(8,128)} %level_hbm.1, f32[8,128]{1,0:T(8,128)} %flow_x_hbm.1, f32[8,128]{1,0:T(8,128)} %flow_y_hbm.1, ...), custom_call_target="tpu_custom_call" | custom-call | tf_op jit(solution)/shard_map/step/pallas_call | solution.py:402
  31.8 0.9 %store.1 = (f32[8,128]{1,0:T(8,128)}, f32[8,128]{1,0:T(8,128)}, f32[8,128]{1,0:T(8,128)}, f32[32,8,128]{2,1,0:T(8,128)}, f32[32,8,128]{2,1,0:T(8,128)}, /*index=5*/f32[32,8,128]{2,1,0:T(8,128)}, f32[32,8,128]{2,1,0:T(8,128)}) custom-call(f32[3,8,128]{2,1,0:T(8,128)S(1)} %get-tuple-element.12.flat, f32[32,8,128]{2,1,0:T(8,128)S(1)} %get-tuple-element.13.x, ...), custom_call_target="tpu_custom_call" | custom-call | tf_op jit(solution)/shard_map/store/pallas_call | solution.py:428

commit v7 on v6

--- a/solution.py
+++ b/solution.py
@@ -165,7 +165,7 @@
     def _():
         pl.semaphore_wait(barrier, awaited)
 
-    for sign, a, o, lead, _ in neighbours[::-1]:
+    for sign, a, o, lead, _ in neighbours[-2:] + neighbours[-3::-1]:
 
         @pl.when(lead == 0)
         def _(sign=sign, a=a, o=o):

time: 32.9 us -> 32.7 us (level)
  no operation moved by 1% of the time
where the time goes in v7:
time: 32.7 us; the launch traced here: 32.6 us
  Pallas kernels  31.9 us (98%)
  between operations  0.64 us (2%)
    pallas_call x1, Pallas kernels, body(): pl.pallas_call(kernel, out_shape=(pltpu.VMEM((3, ROWS, COLS), f32),) + (p...  31.1 us
    pallas_call x1, Pallas kernels, body(): pl.pallas_call(store, out_shape=(flat,) * 3 + (deep,) * 4, in_specs=[pl.B...  0.85 us

profile of v7, /device:TPU:25, one launch (start us, length us, event | category | flops | bytes accessed | tf_op | source)
XLA Modules:
  0.0 32.6 jit_solution(3961851230754657131)
XLA Ops:
  0.6 31.1 %step.1 = (f32[3,8,128]{2,1,0:T(8,128)S(1)}, f32[32,8,128]{2,1,0:T(8,128)S(1)}, f32[32,8,128]{2,1,0:T(8,128)S(1)}, f32[32,8,128]{2,1,0:T(8,128)S(1)}, f32[32,8,128]{2,1,0:T(8,128)S(1)}) custom-call(s32[8,128]{1,0:T(8,128)} %bottom_hbm.1, f32[8,128]{1,0:T(8,128)} %level_hbm.1, f32[8,128]{1,0:T(8,128)} %flow_x_hbm.1, f32[8,128]{1,0:T(8,128)} %flow_y_hbm.1, ...), custom_call_target="tpu_custom_call" | custom-call | tf_op jit(solution)/shard_map/step/pallas_call | solution.py:402
  31.7 0.9 %store.1 = (f32[8,128]{1,0:T(8,128)}, f32[8,128]{1,0:T(8,128)}, f32[8,128]{1,0:T(8,128)}, f32[32,8,128]{2,1,0:T(8,128)}, f32[32,8,128]{2,1,0:T(8,128)}, /*index=5*/f32[32,8,128]{2,1,0:T(8,128)}, f32[32,8,128]{2,1,0:T(8,128)}) custom-call(f32[3,8,128]{2,1,0:T(8,128)S(1)} %get-tuple-element.12.flat, f32[32,8,128]{2,1,0:T(8,128)S(1)} %get-tuple-element.13.x, ...), custom_call_target="tpu_custom_call" | custom-call | tf_op jit(solution)/shard_map/store/pallas_call | solution.py:428
